TPU v7x, 128 devices: a whole 4x4x4 slice. The times are simulated.
128 devices in a mesh: dp: 2 (over core), row: 8 (over x_lo, y), col: 8 (over z, x_hi).
Axes of the slice: x: 4 (x_hi: 2, x_lo: 2; x = x_hi * 2 + x_lo), y: 4, z: 4, core: 2. Of those that a mesh axis runs over, the one named last changes fastest.
Arguments:
- query: bfloat16 [2, 2, 512, 8192], P('dp', None, None, 'col'), may hold values from -6 to 6
- key: bfloat16 [2, 2, 512, 8192], P('dp', None, None, 'col'), may hold values from -6 to 6
- value: bfloat16 [2, 2, 512, 8192], P('dp', None, None, 'row'), may hold values from -6 to 6
- out_grad: bfloat16 [2, 2, 512, 8192], P('dp', None, None, 'row'), may hold values from -6 to 6
- rate: float32 [2, 2, 512], P('dp'), may hold values from 6.1035156e-05 to 0.00048828125
- memory_init: float32 [8192, 8192], P('row', 'col'), may hold values from -0.0625 to 0.0625
- memory_cot: float32 [8192, 8192], P('row', 'col'), may hold values from -128 to 128
Outputs:
- query_grad: bfloat16 [2, 2, 512, 8192], P('dp', None, 'row', 'col')
- key_grad: bfloat16 [2, 2, 512, 8192], P('dp', None, 'row', 'col')
- value_grad: bfloat16 [2, 2, 512, 8192], P('dp', None, 'col', 'row')
- init_grad: float32 [8192, 8192], P('row', 'col')
All inputs are finite; a program needn't handle non-finite values.
Results may differ from a plain program's by a relative error of at most 0.025.
Values may be sent and summed in bfloat16 or wider, within the bound.
A program may use at most 128 MiB of HBM per device.

v0:
```python
import jax
import jax.numpy as jnp
from jax import lax
from jax.sharding import PartitionSpec as P


def on_device(query, key, value, out_grad, rate, memory_init, memory_cot):
    col_count = lax.axis_size("col")
    col_index = lax.axis_index("col")
    row_count_axis = lax.axis_size("row")
    queries = query[0]
    key_blocks = key[0]
    values = value[0]
    grads_out = out_grad[0]
    rates = rate[0]
    blocks = key_blocks.shape[0]
    block_len = key_blocks.shape[1]
    share_len = block_len // col_count
    own_rows = block_len // row_count_axis
    share_start = col_index * share_len
    last_dims = (((1,), (1,)), ((), ()))
    memory = memory_init
    moment = jnp.zeros(memory_init.shape, jnp.float32)
    halves, weights = ([], [])
    for block_index in range(blocks):
        key_rows = key_blocks[block_index]
        value_rows = values[block_index]
        rate_rows = rates[block_index]
        memory_half = memory.astype(jnp.bfloat16)
        partial_err = lax.dot_general(
            key_rows, memory_half, last_dims, preferred_element_type=jnp.float32
        )
        errors = lax.psum(partial_err.astype(jnp.bfloat16), "col").astype(
            jnp.float32
        ) - value_rows.astype(jnp.float32)
        weighted = (rate_rows[:, None] * errors).astype(jnp.bfloat16)
        step_grad = jnp.einsum("ck,cd->kd", weighted, key_rows, preferred_element_type=jnp.float32)
        moment = 0.9 * moment - step_grad
        memory = 0.999 * memory + moment
        halves.append(memory_half)
        weights.append(weighted)
    adjoint = memory_cot
    moment_adj = jnp.zeros(memory_init.shape, jnp.float32)
    value_list = [None] * blocks
    key_list = [None] * blocks
    query_list = [None] * blocks
    err_list = [None] * blocks
    summed_list = [None] * blocks
    for block_index in reversed(range(blocks)):
        query_rows = queries[block_index]
        key_rows = key_blocks[block_index]
        grad_rows = grads_out[block_index]
        rate_rows = rates[block_index]
        memory_half = halves[block_index]
        weighted = weights[block_index]
        summed_adj = adjoint + moment_adj
        summed_half = summed_adj.astype(jnp.bfloat16)
        partial_back = lax.dot_general(
            key_rows, summed_half, last_dims, preferred_element_type=jnp.float32
        )
        err_grad = (
            -(
                rate_rows[:, None]
                * lax.psum(partial_back.astype(jnp.bfloat16), "col").astype(jnp.float32)
            )
        ).astype(jnp.bfloat16)
        err_share = lax.dynamic_slice_in_dim(err_grad, share_start, share_len, 0)
        value_list[block_index] = -err_share
        err_list[block_index] = err_grad
        summed_list[block_index] = summed_half

        def row_terms(
            first_row,
            row_count,
            err_grad=err_grad,
            weighted=weighted,
            grad_rows=grad_rows,
            memory_half=memory_half,
            summed_half=summed_half,
        ):
            key_terms = jnp.dot(
                err_grad, memory_half, preferred_element_type=jnp.float32
            ) - jnp.dot(weighted, summed_half, preferred_element_type=jnp.float32)
            query_terms = jnp.dot(grad_rows, memory_half, preferred_element_type=jnp.float32)
            return jnp.stack([key_terms, query_terms], 1)

        reduced = lax.psum_scatter(
            row_terms(jnp.int32(0), lax.axis_size("row") * own_rows).astype(jnp.bfloat16),
            "row",
            scatter_dimension=0,
            tiled=True,
        ).astype(jnp.float32)
        key_list[block_index] = reduced[:, 0].astype(jnp.bfloat16)
        query_list[block_index] = reduced[:, 1].astype(jnp.bfloat16)
        adjoint = (
            0.999 * adjoint
            + jnp.einsum("ck,cd->kd", grad_rows, query_rows, preferred_element_type=jnp.float32)
            + jnp.einsum("ck,cd->kd", err_grad, key_rows, preferred_element_type=jnp.float32)
        )
        moment_adj = 0.9 * summed_adj
    value_out = jnp.stack(value_list)
    key_out = jnp.stack(key_list)
    query_out = jnp.stack(query_list)
    init_grad = lax.psum(adjoint.astype(jnp.bfloat16), "dp").astype(jnp.float32)
    return (query_out[None], key_out[None], value_out[None], init_grad)


def solution(mesh):
    placed = (
        P("dp", None, None, "col"),
        P("dp", None, None, "col"),
        P("dp", None, None, "row"),
        P("dp", None, None, "row"),
        P("dp", None, None),
        P("row", "col"),
        P("row", "col"),
    )
    return jax.shard_map(
        on_device,
        mesh=mesh,
        in_specs=placed,
        out_specs=(
            P("dp", None, "row", "col"),
            P("dp", None, "row", "col"),
            P("dp", None, "col", "row"),
            P("row", "col"),
        ),
        check_vma=False,
    )
```

profile of v0, /device:TPU:0, one launch (start us, length us, event | category | flops | bytes accessed | tf_op | source)
XLA Modules:
  0.0 381.0 jit_solution(5392149472413771943)
XLA Ops:
  7.2 4.9 %convolution_convert_fusion.3 = bf16[512,1024]{1,0:T(8,128)(2,1)} fusion(bf16[1,2,512,1024]{3,2,1,0:T(8,128)(2,1)} %param.8, f32[1024,1024]{1,0:T(8,128)} %param.12), kind=kOutput, calls=%fused_computation.19 | convolution fusion | flops 1075314688 | bytes 6291456 | tf_op jit(solution)/shard_map/dot_general | solution.py:30
  12.1 2.3 convolution_convert_fusion.5
  15.1 4.8 %fusion.23 = f32[1024,1024]{1,0:T(8,128)} fusion(bf16[1,2,512,1024]{3,2,1,0:T(8,128)(2,1)} %param.7, bf16[1,2,512,1024]{3,2,1,0:T(8,128)(2,1)} %param.10), kind=kOutput, calls=%fused_computation.40 | convolution fusion | flops 1073741824 | bytes 6291456 | tf_op jit(solution)/shard_map/ck,cd->kd/dot_general | solution.py:97
  20.0 104.8 %all-reduce.10.cloned.1.call-done = (bf16[512,1024]{1,0:T(8,128)(2,1)}, bf16[512,1024]{1,0:T(8,128)(2,1)}) async-done(((bf16[512,1024]{1,0:T(8,128)(2,1)}, bf16[512,1024]{1,0:T(8,128)(2,1)}), (bf16[512,1024]{1,0:T(8,128)(2,1)}, bf16[512,1024]{1,0:T(8,128)(2,1)})) %all-reduce.10.cloned.1.call-update) | async-done | bytes 2097168 | tf_op jit(solution)/shard_map/psum | solution.py:33
  124.7 1.5 negate_convert_fusion.1
  126.3 7.2 %add_convert_fusion.2 = (bf16[1024,1024]{1,0:T(8,128)(2,1)S(1)}, f32[1024,1024]{1,0:T(8,128)}) fusion(f32[1024,1024]{1,0:T(8,128)} %param.13, bf16[512,1024]{1,0:T(8,128)(2,1)S(1)} %negate_convert_fusion.1, bf16[1,2,512,1024]{3,2,1,0:T(8,128)(2,1)S(1)} %copy-done.2, f32[1024,1024]{1,0:T(8,128)} %fusion.23), kind=kOutput, calls=%fused_computation.2 | convolution fusion | flops 1080033280 | bytes 16777216 | tf_op jit(solution)/shard_map/ck,cd->kd/dot_general | solution.py:98
  133.5 2.3 fusion.4
  136.0 1.4 copy-done.11
  137.7 1.6 add_convert_fusion.1
  139.3 1.4 copy-done.17
  140.7 2.3 fusion.6
  143.0 1.5 copy-done.13
  144.5 4.5 %fusion.12 = f32[1024,1024]{1,0:T(8,128)} fusion(bf16[1,2,512,1024]{3,2,1,0:T(8,128)(2,1)S(1)} %copy-done.13, bf16[1,2,512,1024]{3,2,1,0:T(8,128)(2,1)} %param.10), kind=kOutput, calls=%fused_computation.29 | convolution fusion | flops 1073741824 | bytes 6291456 | tf_op jit(solution)/shard_map/ck,cd->kd/dot_general | solution.py:97
  149.0 100.0 %all-reduce.8.cloned.1.call-done = (bf16[512,1024]{1,0:T(8,128)(2,1)}, bf16[512,1024]{1,0:T(8,128)(2,1)}) async-done(((bf16[512,1024]{1,0:T(8,128)(2,1)}, bf16[512,1024]{1,0:T(8,128)(2,1)}), (bf16[512,1024]{1,0:T(8,128)(2,1)}, bf16[512,1024]{1,0:T(8,128)(2,1)})) %all-reduce.8.cloned.1.call-update) | async-done | bytes 2097168 | tf_op jit(solution)/shard_map/psum | solution.py:33
  249.0 1.7 negate_convert_fusion
  250.9 6.3 %add_convert_fusion = bf16[1024,1024]{1,0:T(8,128)(2,1)} fusion(f32[1024,1024]{1,0:T(8,128)} %fusion.12, f32[1024,1024]{1,0:T(8,128)} %get-tuple-element.15, bf16[512,1024]{1,0:T(8,128)(2,1)S(1)} %negate_convert_fusion, bf16[1,2,512,1024]{3,2,1,0:T(8,128)(2,1)S(1)} %copy-done.3), kind=kOutput, calls=%fused_computation | convolution fusion | flops 1077936128 | bytes 12582912 | tf_op jit(solution)/shard_map/ck,cd->kd/dot_general | solution.py:98
  257.5 3.0 fusion.51
  260.5 1.3 fusion.7
  261.8 1.0 copy-done.1
  263.1 1.3 fusion.9
  264.4 1.5 pad_maximum_fusion.1
  266.0 4.2 %fusion.5 = bf16[512,1,1024]{2,0,1:T(8,128)(2,1)S(1)} fusion(bf16[1,2,512,1024]{3,2,1,0:T(8,128)(2,1)} %param.10, f32[1024,1024]{1,0:T(8,128)} %param.12), kind=kOutput, calls=%fused_computation.23 | convolution fusion | flops 1075314688 | bytes 6291456 | tf_op jit(solution)/shard_map/dot_general | solution.py:84
  270.2 1.3 fusion.46
  272.6 1.3 fusion.8
  274.0 1.5 pad_maximum_fusion
  276.3 6.1 %all-reduce.6.cloned.1.call-done = bf16[1024,1024]{1,0:T(8,128)(2,1)} async-done(((bf16[1024,1024]{1,0:T(8,128)(2,1)}), bf16[1024,1024]{1,0:T(8,128)(2,1)}) %all-reduce.6.cloned.1.call-update) | async-done | bytes 2097168 | tf_op jit(solution)/shard_map/psum | solution.py:104
  282.4 4.1 %convert_element_type.147 = f32[1024,1024]{1,0:T(8,128)} convert(bf16[1024,1024]{1,0:T(8,128)(2,1)} %all-reduce.6.cloned.1.call-done) | non-fusion elementwise | flops 1048576 | bytes 6291456 | tf_op jit(solution)/shard_map/convert_element_type | solution.py:104
  286.5 42.4 %reduce-scatter.5.cloned.1.call-done = bf16[64,2,1024]{2,0,1:T(8,128)(2,1)} async-done(((bf16[512,2,1024]{2,0,1:T(8,128)(2,1)}), bf16[64,2,1024]{2,0,1:T(8,128)(2,1)}) %reduce-scatter.5.cloned.1.call-update) | async-done | bytes 262160 | tf_op jit(solution)/shard_map/reduce_scatter | solution.py:87
  328.8 1.0 slice_bitcast_fusion
  329.8 42.8 %reduce-scatter.3.cloned.1.call-done = bf16[64,2,1024]{2,0,1:T(8,128)(2,1)} async-done(((bf16[512,2,1024]{2,0,1:T(8,128)(2,1)}), bf16[64,2,1024]{2,0,1:T(8,128)(2,1)}) %reduce-scatter.3.cloned.1.call-update) | async-done | bytes 262160 | tf_op jit(solution)/shard_map/reduce_scatter | solution.py:87
  372.6 1.0 slice_bitcast_fusion.1
  373.6 0.8 maximum_bitcast_fusion
  (47 shorter events, 4.0 us)
Async XLA Ops:
  7.2 5.0 %copy-start.2 = (bf16[1,2,512,1024]{3,2,1,0:T(8,128)(2,1)S(1)}, bf16[1,2,512,1024]{3,2,1,0:T(8,128)(2,1)}, u32[]{:S(2)}) copy-start(bf16[1,2,512,1024]{3,2,1,0:T(8,128)(2,1)} %param.8) | copy-start | bytes 6291460
  7.2 117.6 %all-reduce.10.cloned.1.call-start = ((), (), s32[]{:S(2)}) async-start(), calls=%async_computation.6 | async-start | bytes 4194304 | tf_op jit(solution)/shard_map/psum | solution.py:33
  7.2 4.9 %copy-start = (f32[1024,1024]{1,0:T(8,128)S(1)}, f32[1024,1024]{1,0:T(8,128)}, u32[]{:S(2)}) copy-start(f32[1024,1024]{1,0:T(8,128)} %param.13) | copy-start | bytes 12582916
  14.4 0.7 copy-start.10
  14.5 234.6 %all-reduce.8.cloned.1.call-start = ((), (), s32[]{:S(2)}) async-start(), calls=%async_computation.5 | async-start | bytes 4194304 | tf_op jit(solution)/shard_map/psum | solution.py:33
  133.4 2.4 copy-start.4
  133.4 2.5 copy-start.7
  133.5 4.0 %copy-start.11 = (f32[1024,1024]{1,0:T(8,128)S(1)}, f32[1024,1024]{1,0:T(8,128)}, u32[]{:S(2)}) copy-start(f32[1024,1024]{1,0:T(8,128)} %param.12) | copy-start | bytes 12582916
  133.5 4.2 %copy-start.15 = (bf16[512,1024]{1,0:T(8,128)(2,1)S(1)}, bf16[512,1024]{1,0:T(8,128)(2,1)}, u32[]{:S(2)}) copy-start(bf16[512,1024]{1,0:T(8,128)(2,1)} %get-tuple-element.6) | copy-start | bytes 3145732
  139.3 1.4 copy-start.17
  143.0 1.6 copy-start.13
  143.0 139.4 %all-reduce.6.cloned.1.call-start = ((), (), s32[]{:S(2)}) async-start(), calls=%async_computation.4 | async-start | bytes 4194304 | tf_op jit(solution)/shard_map/psum | solution.py:104
  249.0 1.9 copy-start.3
  257.2 71.6 %reduce-scatter.5.cloned.1.call-start = ((), (), s32[]{:S(2)}) async-start(), calls=%async_computation.3 | async-start | bytes 2359296 | tf_op jit(solution)/shard_map/reduce_scatter | solution.py:87
  257.5 3.0 copy-start.14
  257.5 3.0 copy-start.18
  257.5 4.3 %copy-start.8 = (bf16[1,2,512,1024]{3,2,1,0:T(8,128)(2,1)S(1)}, bf16[1,2,512,1024]{3,2,1,0:T(8,128)(2,1)}, u32[]{:S(2)}) copy-start(bf16[1,2,512,1024]{3,2,1,0:T(8,128)(2,1)} %param.9) | copy-start | bytes 6291460
  260.5 2.3 copy-start.1
  260.5 2.5 copy-start.6
  265.9 106.7 %reduce-scatter.3.cloned.1.call-start = ((), (), s32[]{:S(2)}) async-start(), calls=%async_computation.2 | async-start | bytes 2359296 | tf_op jit(solution)/shard_map/reduce_scatter | solution.py:87
  266.0 4.2 %copy-start.12 = (f32[1024,1024]{1,0:T(8,128)S(1)}, f32[1024,1024]{1,0:T(8,128)}, u32[]{:S(2)}) copy-start(f32[1024,1024]{1,0:T(8,128)} %param.12) | copy-start | bytes 12582916
  270.1 1.6 copy-start.5
  270.2 2.2 copy-start.9
  270.2 2.5 copy-start.16
Sparse Core Ops, SparseCore 0:
  14.6 110.0 all-reduce.9
  143.1 105.8 all-reduce.7
  257.4 25.0 all-reduce.5
  284.8 43.9 reduce-scatter.4
  331.2 41.3 reduce-scatter.2
where the time goes:
time: 381 us
  waiting for transfers between devices  296 us (78%)
  matrix products  48.6 us (13%)
  between operations  14 us (4%)
  other arithmetic  11.9 us (3%)
  local copies, waits for them, and re-layouts  10 us (3%)
    psum x2, waiting for transfers between devices, on_device(): lax.psum(partial_err.astype(jnp.bfloat16), 'col').astype(jnp.float32)  205 us
    reduce_scatter x2, waiting for transfers between devices, on_device(): lax.psum_scatter(row_terms(jnp.int32(0), lax.axis_size('row') * own_rows)...  85.1 us
    dot_general x2, matrix products, on_device(): jnp.einsum('ck,cd->kd', err_grad, key_rows, preferred_element_type=jnp.fl...  13.4 us
    dot_general x2, matrix products, on_device(): jnp.einsum('ck,cd->kd', grad_rows, query_rows, preferred_element_type=jnp...  9.32 us
    unnamed x38, local copies, waits for them, and re-layouts  8.05 us
  transfers between devices with their start and end apart: 5, of which 5 were waited for; matrix products, arithmetic and copies ran while one was open for 8% of the time, Pallas kernels for 0%

commit v1 on v0

v1 whole, which is shorter than its diff:
```python
import functools

import jax
import jax.numpy as jnp
from jax import lax
from jax.experimental import pallas as pl
from jax.experimental.pallas import tpu as pltpu
from jax.sharding import PartitionSpec as P

MESH = pl.DeviceIdType.MESH
BF, F32 = jnp.bfloat16, jnp.float32
W = 1024
SH = 64
NJ = 4
CW, RW = W // NJ, SH // NJ
ALL = slice(0, W)
X_FIRST = frozenset([(0, 1), (1, 1), (1, 3), (2, 1), (3, 1)])
UNIT_US = 22.3
HOP_US = 1.0
NT = (((1,), (1,)), ((), ()))
TN = (((0,), (0,)), ((), ()))


class Task:
    def __init__(self, name, needs, waits, cost, body, starts, rank):
        self.name, self.needs, self.waits, self.cost = name, needs, waits, cost
        self.body, self.starts, self.rank = body, starts, rank


def order_tasks(tasks, links, sizes):
    free, arrive, done, now = {}, {}, {}, 0.0
    left, result = list(tasks), []
    while left:
        best = None
        for task in left:
            if any(n not in done for n in task.needs) or any(w not in arrive for w in task.waits):
                continue
            ready = max([now] + [done[n] for n in task.needs] + [arrive[w] for w in task.waits])
            key = (ready, task.rank)
            if best is None or key < best[0]:
                best = (key, task)
        (ready, _), task = best
        now = ready + task.cost
        done[task.name] = now
        for copy in task.starts:
            link = links[copy]
            begin = max(now, free.get(link, 0.0))
            free[link] = begin + sizes[copy]
            arrive[copy] = free[link] + HOP_US
        left.remove(task)
        result.append(task)
    return result, now


def kernel(
    q_hbm, k_hbm, v_hbm, y_hbm, r_ref, m_hbm, c_hbm,
    qg_ref, kg_ref, vg_ref, ig_hbm,
    kb, qb, yb, vb, mf, cf, mh0, mh1, ch, ph0, part, full, rbuf, part2, rbuf2, abf, arec, rc,
    ssem, rsem, lsem,
):
    dp, row, col = lax.axis_index("dp"), lax.axis_index("row"), lax.axis_index("col")
    z, xh = col // 2, col % 2
    xl, y = row // 4, row % 4
    zp, zm, z2, xo = (z + 1) % 4, (z + 3) % 4, (z + 2) % 4, 1 - xh
    yp, ym, y2, lo = (y + 1) % 4, (y + 3) % 4, (y + 2) % 4, 1 - xl
    device = {
        "z+": (dp, row, zp * 2 + xh),
        "z-": (dp, row, zm * 2 + xh),
        "xh": (dp, row, z * 2 + xo),
        "y+": (dp, xl * 4 + yp, col),
        "y-": (dp, xl * 4 + ym, col),
        "xl": (dp, lo * 4 + y, col),
        "dp": (1 - dp, row, col),
    }

    loads = {}

    def load(name, src, dst):
        copy = pltpu.make_async_copy(src, dst, lsem.at[len(loads)])
        copy.start()
        loads[name] = copy

    def rows_of(g):
        return pl.ds(g * CW, CW)

    load("K1", k_hbm.at[0, 1], kb.at[1])
    for g in range(NJ):
        load(("C", g), c_hbm.at[rows_of(g)], cf.at[rows_of(g)])
    load("K0", k_hbm.at[0, 0], kb.at[0])
    for g in range(NJ):
        load(("M", g), m_hbm.at[rows_of(g)], mf.at[rows_of(g)])
    load("V", v_hbm.at[0, :, col], vb)
    load("Y0", y_hbm.at[0, 0], yb.at[0])
    load("Y1", y_hbm.at[0, 1], yb.at[1])
    load("Q1", q_hbm.at[0, 1], qb.at[1])
    load("Q0", q_hbm.at[0, 0], qb.at[0])
    loaded = set()

    def need(*names):
        for name in names:
            if name not in loaded:
                loaded.add(name)
                loads[name].wait()

    barrier = pltpu.get_barrier_semaphore()
    for partner in device.values():
        pl.semaphore_signal(barrier, inc=1, device_id=partner, device_id_type=MESH)

    at = lax.broadcasted_iota(jnp.int32, (SH, 8 * SH), 1)
    own = lax.broadcasted_iota(jnp.int32, (SH, 8 * SH), 0) + col * SH
    for b in range(2):
        picked = jnp.where(at == own, jnp.broadcast_to(r_ref[0, b : b + 1, :], (SH, 8 * SH)), 0.0)
        rc[b] = jnp.broadcast_to(jnp.sum(picked, axis=1, keepdims=True), (SH, 128))

    copies, links, sizes = {}, {}, {}

    def copy(name, link, src, dst, units):
        index = len(copies)
        copies[name] = pltpu.make_async_remote_copy(
            src_ref=src, dst_ref=dst, send_sem=ssem.at[index], recv_sem=rsem.at[index],
            device_id=device[link], device_id_type=MESH,
        )
        links[name] = "x" if link in ("xh", "xl") else link
        sizes[name] = units * (UNIT_US if link != "dp" else 1.2)

    tasks = []

    def task(name, needs, waits, cost, body, starts, rank):
        tasks.append(Task(name, needs, waits, cost, body, starts, rank))

    def f32(ref, *index):
        return ref[index].astype(F32)

    def finish(q, cs, rs, total):
        b = 1 if q in (0, 3) else 0
        wide = total.shape[1]
        rate = jnp.broadcast_to(rc[b, rs, 0:1], total.shape)
        if q in (0, 2):
            scaled = (rate * total).astype(BF)
            vg_ref[0, b, rs, cs] = scaled
            full[q, z, xh, rs, cs] = -scaled
        else:
            full[q, z, xh, rs, cs] = (rate * (total - f32(vb, b, rs, cs))).astype(BF)

    def reduce_job(tag, q, rs, cs, rank, P4, R, first, pieces, names, after, after_cost, after_starts):
        ring, ahead, behind, far, mine, other = pieces
        up, down, side = names
        u = (rs.stop - rs.start) * (cs.stop - cs.start) / (SH * W) / 8.0

        def part_at(i, half):
            return P4(i, half)

        def slot(k):
            return R.at[q, k, rs, cs]

        n = lambda k: (tag, q, rank, k)
        copy(n("D1p"), up, part_at(far, mine), slot(0), u)
        copy(n("D1m"), down, part_at(far, other), slot(1), u)
        copy(n("D2pA"), up, part_at(ahead, mine), slot(2), u)
        copy(n("D2pB"), up, part_at(ahead, other), slot(3), u)
        copy(n("D2mA"), down, part_at(behind, mine), slot(4), u)
        copy(n("D2mB"), down, part_at(behind, other), slot(5), u)
        copy(n("DX"), side, part_at(ring, other), slot(6), u)

        def add(ref, *slots):
            total = ref[...].astype(F32)
            for k in slots:
                total = total + R[q, k, rs, cs].astype(F32)
            return total

        def s1p():
            ref = part_at(ahead, mine)
            ref[...] = add(ref, 0).astype(BF)

        def s1m():
            ref = part_at(behind, other)
            ref[...] = add(ref, 1).astype(BF)

        def s2():
            ref = part_at(ring, other)
            ref[...] = add(ref, 3, 5).astype(BF)

        def s3():
            after(rs, cs, add(part_at(ring, mine), 2, 4, 6))

        vpu = u * 8 * 0.15 + 0.05
        task(n("s1p"), [first], [n("D1p")], vpu, s1p, [n("D2pA")], rank)
        task(n("s1m"), [first], [n("D1m")], vpu, s1m, [n("D2mB")], rank)
        task(n("s2"), [n("s1p"), n("s1m")], [n("D2pB"), n("D2mB")], vpu, s2, [n("DX")], rank)
        task(n("s3"), [n("s2")], [n("D2pA"), n("D2mA"), n("DX")], vpu + after_cost, s3, after_starts, rank)
        return [n("D1p"), n("D1m"), n("D2pB"), n("D2mA")], n("s3")

    def col_z(q, rs, cs, rank, first):
        u = (rs.stop - rs.start) * (cs.stop - cs.start) / (SH * W) / 8.0
        tag = "cz"
        n = lambda k: (tag, q, rank, k)

        def P4(i, half):
            return part.at[q, i, half, rs, cs]

        def F4(i, half):
            return full.at[q, i, half, rs, cs]

        copy(n("GX"), "xh", F4(z, xh), F4(z, xh), u)
        copy(n("Gop"), "z+", F4(z, xh), F4(z, xh), u)
        copy(n("Gom"), "z-", F4(z, xh), F4(z, xh), u)
        copy(n("Gtp"), "z+", F4(z, xo), F4(z, xo), u)
        copy(n("Gtm"), "z-", F4(z, xo), F4(z, xo), u)
        copy(n("Fp"), "z+", F4(zm, xh), F4(zm, xh), u)
        copy(n("Fm"), "z-", F4(zp, xo), F4(zp, xo), u)
        starts, last = reduce_job(
            tag, q, rs, cs, rank, P4, rbuf, first, (z, zp, zm, z2, xh, xo), ("z+", "z-", "xh"),
            lambda rs, cs, total: finish(q, cs, rs, total), 0.1, [n("GX"), n("Gop"), n("Gom")],
        )
        task(n("s4"), [last], [n("GX")], 0.05, None, [n("Gtp"), n("Gtm")], rank)
        task(n("s5p"), [last], [n("Gop")], 0.05, None, [n("Fp")], rank)
        task(n("s5m"), [last], [n("Gtm")], 0.05, None, [n("Fm")], rank)
        task(n("end"), [n("s4"), n("s5p"), n("s5m")], [n("Gom"), n("Gtp"), n("Fp"), n("Fm")], 0.05, None, [], rank)
        return starts, n("end")

    def col_x(q, rs, cs, rank, first):
        u = (rs.stop - rs.start) * (cs.stop - cs.start) / (SH * W) / 8.0
        half = (cs.stop - cs.start) // 2
        cl, cr = slice(cs.start, cs.start + half), slice(cs.start + half, cs.stop)
        n = lambda k: ("cx", q, rank, k)

        def P3(i, c):
            return part.at[q, i, xh, rs, c]

        def F3(i, c):
            return full.at[q, i, xh, rs, c]

        def slot(k, c):
            return rbuf.at[q, k, rs, c]

        copy(n("DX"), "xh", part.at[q, :, xo, rs, cs], rbuf.at[q, pl.ds(0, 4), rs, cs], 4 * u)
        copy(n("D1p"), "z+", P3(z2, cl), slot(4, cl), u / 2)
        copy(n("D1m"), "z-", P3(z2, cr), slot(4, cr), u / 2)
        copy(n("D2pL"), "z+", P3(zp, cl), slot(5, cl), u / 2)
        copy(n("D2pR"), "z+", P3(zp, cr), slot(5, cr), u / 2)
        copy(n("D2mL"), "z-", P3(zm, cl), slot(6, cl), u / 2)
        copy(n("D2mR"), "z-", P3(zm, cr), slot(6, cr), u / 2)
        copy(n("Gp"), "z+", F3(z, cs), F3(z, cs), u)
        copy(n("Gm"), "z-", F3(z, cs), F3(z, cs), u)
        copy(n("Fp"), "z+", F3(zm, cl), F3(zm, cl), u / 2)
        copy(n("Fm"), "z-", F3(zp, cr), F3(zp, cr), u / 2)
        copy(n("X0"), "xh", F3(z, cs), F3(z, cs), u)
        copy(n("Xm"), "xh", F3(zm, cs), F3(zm, cs), u)
        copy(n("Xp"), "xh", F3(zp, cs), F3(zp, cs), u)
        copy(n("X2"), "xh", F3(z2, cs), F3(z2, cs), u)

        def s1():
            for i in range(4):
                part[q, i, xh, rs, cs] = (f32(part, q, i, xh, rs, cs) + f32(rbuf, q, i, rs, cs)).astype(BF)

        def s2p():
            part[q, zp, xh, rs, cl] = (f32(part, q, zp, xh, rs, cl) + f32(rbuf, q, 4, rs, cl)).astype(BF)

        def s2m():
            part[q, zm, xh, rs, cr] = (f32(part, q, zm, xh, rs, cr) + f32(rbuf, q, 4, rs, cr)).astype(BF)

        def s3():
            finish(q, cs, rs, f32(part, q, z, xh, rs, cs) + f32(rbuf, q, 5, rs, cs) + f32(rbuf, q, 6, rs, cs))

        vpu = u * 8 * 0.15 + 0.05
        task(n("s1"), [first], [n("DX")], 2 * vpu, s1, [n("D1p"), n("D1m"), n("D2pR"), n("D2mL")], rank)
        task(n("s2p"), [n("s1")], [n("D1p")], vpu, s2p, [n("D2pL")], rank)
        task(n("s2m"), [n("s1")], [n("D1m")], vpu, s2m, [n("D2mR")], rank)
        task(n("s3"), [n("s2p"), n("s2m")], [n("D2pL"), n("D2pR"), n("D2mL"), n("D2mR")], vpu + 0.1, s3,
             [n("Gp"), n("Gm"), n("X0")], rank)
        task(n("s4p"), [n("s3")], [n("Gp")], 0.05, None, [n("Fp"), n("Xm")], rank)
        task(n("s4m"), [n("s3")], [n("Gm")], 0.05, None, [n("Fm"), n("Xp")], rank)
        task(n("s5"), [n("s4p"), n("s4m")], [n("Fp"), n("Fm")], 0.05, None, [n("X2")], rank)
        task(n("end"), [n("s5")], [n("X0"), n("Xm"), n("Xp"), n("X2")], 0.05, None, [], rank)
        return [n("DX")], n("end")

    def row_job(u, rs, cs, rank, first):
        def P4(i, half):
            return part2.at[u, half, i, rs, cs]

        def store(rs, cs, total):
            ref, b = ((qg_ref, 0), (qg_ref, 1), (kg_ref, 0), (kg_ref, 1))[u]
            ref[0, b, rs, cs] = total.astype(BF)

        return reduce_job(
            "r", u, rs, cs, rank, P4, rbuf2, first, (y, yp, ym, y2, xl, lo), ("y+", "y-", "xl"), store, 0.0, [],
        )

    def dot(a, b, dims=None):
        if dims is None:
            return jnp.dot(a, b, preferred_element_type=F32)
        return lax.dot_general(a, b, dims, preferred_element_type=F32)

    def whole(ref, *index):
        return ref[index].reshape(8 * SH, -1)

    def some(ref, *index):
        return ref[index].reshape(8 * RW, W)

    ends = [[None] * NJ for _ in range(4)]
    everything = slice(0, SH)
    full_cols = slice(0, W)

    def cols(g):
        return slice(g * CW, (g + 1) * CW)

    def toks(k):
        return slice(k * RW, (k + 1) * RW)

    def spread(q, block, width, value, rs, cs):
        part[q, :, :, rs, cs] = value.astype(BF).reshape(4, 2, rs.stop - rs.start, cs.stop - cs.start)

    def phase_a(q, g, rank):
        b, src, half = (1, cf, ch) if q == 0 else (0, mf, mh0)
        rs, cs = everything, cols(g)
        name = ("P", q, g)

        def body():
            need("K1" if q == 0 else "K0", ("C" if q == 0 else "M", g))
            half[cs, :] = src[cs, :].astype(BF)
            spread(q, g, CW, dot(whole(kb, b), half[cs, :], NT), rs, cs)

        make = col_x if (q, g) in X_FIRST else col_z
        starts, ends[q][g] = make(q, rs, cs, rank, name)
        task(name, [], [], 0.45, body, starts, rank)

    for i, (q, g) in enumerate([(0, g) for g in range(NJ)] + [(1, g) for g in range(NJ)]):
        phase_a(q, g, i)

    def project_update(g):
        cs = cols(g)

        def body():
            need("Y1", "Q1", "K1")
            step = dot(full[0, :, :, :, cs].reshape(8 * SH, CW), whole(kb, 1), TN)
            step = step + dot(yb[1, :, :, cs].reshape(8 * SH, CW), whole(qb, 1), TN)
            before = cf[cs, :]
            adjoint = 0.999 * before + step
            cf[cs, :] = adjoint
            ph0[cs, :] = (adjoint + 0.9 * before).astype(BF)

        task(("PU", g), [ends[0][g]], [], 1.0, body, [], 7.5)

    def memory_update(g):
        cs = cols(g)

        def body():
            need("K0")
            step = dot(full[1, :, :, :, cs].reshape(8 * SH, CW), whole(kb, 0), TN)
            mh1[cs, :] = (0.999 * mf[cs, :] - step).astype(BF)

        task(("MU", g), [ends[1][g]], [], 0.6, body, [], 8.5)

    for g in range(NJ):
        project_update(g)
        memory_update(g)
    all_pu = [("PU", g) for g in range(NJ)]
    all_mu = [("MU", g) for g in range(NJ)]

    def query_part(u, g, rank):
        mem = mh0 if u == 0 else mh1
        rs, cs = everything, cols(g)
        name = ("QP", u, g)

        def body():
            need("Y%d" % u)
            value = dot(whole(yb, u), mem[:, cs])
            part2[u, :, :, rs, cs] = value.astype(BF).reshape(2, 4, SH, CW)

        starts, _ = row_job(u, rs, cs, rank, name)
        deps = [("P", 1, g) for g in range(NJ)] if u == 0 else all_mu
        task(name, deps, [], 0.4, body, starts, rank)

    for g in range(NJ):
        query_part(0, g, 20 + g)
        query_part(1, g, 24 + g)

    def phase_b(q, k, rank):
        b, half, deps = (0, ph0, all_pu) if q == 2 else (1, mh1, all_mu)
        rs, cs = toks(k), full_cols
        name = ("P", q, k)

        def body():
            need("K%d" % b)
            lhs = some(kb, b, slice(None), rs)
            for n in range(NJ):
                spread(q, n, CW, dot(lhs, half[cols(n), :], NT), rs, cols(n))

        make = col_x if (q, k) in X_FIRST else col_z
        starts, ends[q][k] = make(q, rs, cs, rank, name)
        task(name, deps, [], 0.7, body, starts, rank)

    for i, (q, k) in enumerate([(2, k) for k in range(NJ)] + [(3, k) for k in range(NJ)]):
        phase_b(q, k, 8 + i)

    def key_part(u, k, rank):
        rs = toks(k)
        f, w, mem, proj = (2, 1, mh0, ph0) if u == 2 else (0, 3, mh1, ch)
        name = ("KP", u, k)

        def body():
            err, wgt = some(full, f, slice(None), slice(None), rs), some(full, w, slice(None), slice(None), rs)
            for n in range(NJ):
                value = dot(err, mem[:, cols(n)]) - dot(wgt, proj[:, cols(n)])
                part2[u, :, :, rs, cols(n)] = value.astype(BF).reshape(2, 4, RW, CW)

        starts, _ = row_job(u, rs, full_cols, rank, name)
        deps = [ends[2][k]] + all_pu + all_mu if u == 2 else [ends[3][k]] + all_pu + all_mu
        task(name, deps, [], 1.2, body, starts, rank)

    for k in range(NJ):
        key_part(2, k, 17 + k / 10)
        key_part(3, k, 18 + k / 10)

    outs = []

    def adjoint_early(g):
        cs = cols(g)

        def body():
            need("Y0", "Q0")
            cf[cs, :] = 0.999 * cf[cs, :] + dot(yb[0, :, :, cs].reshape(8 * SH, CW), whole(qb, 0), TN)

        task(("AE", g), [("PU", g)], [], 0.6, body, [], 30)

    def adjoint_late(g):
        cs = cols(g)

        def body():
            step = dot(full[2, :, :, :, cs].reshape(8 * SH, CW), whole(kb, 0), TN)
            abf[cs, :] = (cf[cs, :] + step).astype(BF)

        copy(("A", g), "dp", abf.at[rows_of(g)], arec.at[rows_of(g)], 0.5)
        task(("AL", g), [("AE", g)] + ends[2], [], 0.6, body, [("A", g)], 19)

        def total():
            cf[cs, :] = abf[cs, :].astype(F32) + arec[cs, :].astype(F32)
            out = pltpu.make_async_copy(cf.at[rows_of(g)], ig_hbm.at[rows_of(g)], lsem.at[len(loads) + g])
            out.start()
            outs.append(out)

        task(("AT", g), [("AL", g)], [("A", g)], 0.3, total, [], 31)

    for g in range(NJ):
        adjoint_early(g)
    for g in range(NJ):
        adjoint_late(g)

    order, _ = order_tasks(tasks, links, sizes)
    pl.semaphore_wait(barrier, len(device))
    need("V")
    for item in order:
        for name in item.waits:
            copies[name].wait_recv()
        if item.body is not None:
            item.body()
        for name in item.starts:
            copies[name].start()
    for name in copies:
        copies[name].wait_send()
    for out in outs:
        out.wait()


def on_device(query, key, value, out_grad, rate, memory_init, memory_cot):
    shared = (1, 2, 8, SH, W)
    vm = pltpu.VMEM
    n_copies = 16 * 15 + 16 * 7 + NJ
    outs = pl.pallas_call(
        kernel,
        out_shape=(
            jax.ShapeDtypeStruct((1, 2, SH, W), BF),
            jax.ShapeDtypeStruct((1, 2, SH, W), BF),
            jax.ShapeDtypeStruct((1, 2, SH, W), BF),
            jax.ShapeDtypeStruct((W, W), F32),
        ),
        in_specs=[pl.BlockSpec(memory_space=pl.ANY)] * 4
        + [pl.BlockSpec(memory_space=vm)]
        + [pl.BlockSpec(memory_space=pl.ANY)] * 2,
        out_specs=(
            pl.BlockSpec(memory_space=vm),
            pl.BlockSpec(memory_space=vm),
            pl.BlockSpec(memory_space=vm),
            pl.BlockSpec(memory_space=pl.ANY),
        ),
        scratch_shapes=[
            vm((2, 8, SH, W), BF),
            vm((2, 8, SH, W), BF),
            vm((2, 8, SH, W), BF),
            vm((2, SH, W), BF),
            vm((W, W), F32),
            vm((W, W), F32),
            vm((W, W), BF),
            vm((W, W), BF),
            vm((W, W), BF),
            vm((W, W), BF),
            vm((4, 4, 2, SH, W), BF),
            vm((4, 4, 2, SH, W), BF),
            vm((4, 7, SH, W), BF),
            vm((4, 2, 4, SH, W), BF),
            vm((4, 7, SH, W), BF),
            vm((W, W), BF),
            vm((W, W), BF),
            vm((2, SH, 128), F32),
            pltpu.SemaphoreType.DMA((n_copies,)),
            pltpu.SemaphoreType.DMA((n_copies,)),
            pltpu.SemaphoreType.DMA((32,)),
        ],
        compiler_params=pltpu.CompilerParams(
            collective_id=0, has_side_effects=True, vmem_limit_bytes=62 * 2**20
        ),
        name="memory_backward",
    )(
        query.reshape(shared), key.reshape(shared), value.reshape(shared), out_grad.reshape(shared), rate,
        memory_init, memory_cot,
    )
    return outs


def solution(mesh):
    placed = (
        P("dp", None, None, "col"),
        P("dp", None, None, "col"),
        P("dp", None, None, "row"),
        P("dp", None, None, "row"),
        P("dp", None, None),
        P("row", "col"),
        P("row", "col"),
    )
    return jax.shard_map(
        on_device,
        mesh=mesh,
        in_specs=placed,
        out_specs=(
            P("dp", None, "row", "col"),
            P("dp", None, "row", "col"),
            P("dp", None, "col", "row"),
            P("row", "col"),
        ),
        check_vma=False,
    )
```

time: 381 us -> 128 us (0.34)
  waiting for transfers between devices: 296 us -> 0 us
  Pallas kernels: 0 us -> 118 us
  matrix products: 48.6 us -> 0 us
  between operations: 14 us -> 0.64 us
  other arithmetic: 11.9 us -> 0 us
    psum x3 -> x0, waiting for transfers between devices: 211 us -> none  [the longest x2 205 us: on_device(): lax.psum(partial_err.astype(jnp.bfloat16), 'col').astype(jnp.float32)]
    pallas_call x0 -> x1, Pallas kernels: none -> 118 us  [on_device(): pl.pallas_call(kernel, out_shape=(jax.ShapeDtypeStruct((1, 2, SH, W), BF)...]
    reduce_scatter x2 -> x0, waiting for transfers between devices: 85.1 us -> none  [on_device(): lax.psum_scatter(row_terms(jnp.int32(0), lax.axis_size('row') * own_rows)...]
    dot_general x15 -> x0, matrix products: 48.6 us -> none  [the longest x2 13.4 us: on_device(): jnp.einsum('ck,cd->kd', err_grad, key_rows, preferred_element_type=jnp.fl...]
    convert_element_type x3 -> x0, other arithmetic: 7.27 us -> none  [the longest x1 4.07 us: on_device(): init_grad = lax.psum(adjoint.astype(jnp.bfloat16), 'dp').astype(jnp.float32)]
    unnamed x38 -> x4, local copies, waits for them, and re-layouts: 8.05 us -> 9.79 us
  transfers between devices with their start and end apart: 5 -> 0, of which waited for: 5 -> 0; matrix products, arithmetic and copies ran while one was open for 8% -> 0% of each run, Pallas kernels for 0% -> 0%
where the time goes in v1:
time: 128 us
  Pallas kernels  118 us (92%)
  local copies, waits for them, and re-layouts  9.79 us (8%)
    pallas_call x1, Pallas kernels, on_device(): pl.pallas_call(kernel, out_shape=(jax.ShapeDtypeStruct((1, 2, SH, W), BF)...  118 us
    unnamed x4, local copies, waits for them, and re-layouts  9.79 us

profile of v1, /device:TPU:0, one launch (start us, length us, event | category | flops | bytes accessed | tf_op | source)
XLA Modules:
  0.0 128.0 jit_solution(2001618375521864765)
XLA Ops:
  0.6 117.6 %memory_backward.1 = (bf16[1,2,64,1024]{3,2,1,0:T(8,128)(2,1)}, bf16[1,2,64,1024]{3,2,1,0:T(8,128)(2,1)}, bf16[1,2,64,1024]{3,2,1,0:T(8,128)(2,1)}, f32[1024,1024]{1,0:T(8,128)}) custom-call(bf16[1,2,8,64,1024]{4,3,2,1,0:T(8,128)(2,1)} %bitcast.4, bf16[1,2,8,64,1024]{4,3,2,1,0:T(8,128)(2,1)} %bitcast.5, bf16[1,2,8,64,1024]{4,3,2,1,0:T(8,128)(2,1)} %bitcast.6, ...), custom_call_target="tpu_custom_call" | custom-call | tf_op jit(solution)/shard_map/memory_backward/pallas_call | solution.py:469
  118.2 1.7 %copy.15 = bf16[1,2,64,1024]{3,2,1,0:T(8,128)(2,1)} copy(bf16[1,2,64,1024]{3,2,1,0:T(8,128)(2,1)} %get-tuple-element.8) | data formatting | bytes 524288
  119.9 1.7 %copy.16 = bf16[1,2,64,1024]{3,2,1,0:T(8,128)(2,1)} copy(bf16[1,2,64,1024]{3,2,1,0:T(8,128)(2,1)} %get-tuple-element.9) | data formatting | bytes 524288
  121.6 1.7 %copy.17 = bf16[1,2,64,1024]{3,2,1,0:T(8,128)(2,1)} copy(bf16[1,2,64,1024]{3,2,1,0:T(8,128)(2,1)} %get-tuple-element.10) | data formatting | bytes 524288
  123.3 4.8 %copy.18 = f32[1024,1024]{1,0:T(8,128)} copy(f32[1024,1024]{1,0:T(8,128)} %get-tuple-element.11) | data formatting | bytes 8388608

commit v2 on v1

v2 whole, which is shorter than its diff:
```python
import functools

import jax
import jax.numpy as jnp
from jax import lax
from jax.experimental import pallas as pl
from jax.experimental.pallas import tpu as pltpu
from jax.sharding import PartitionSpec as P

MESH = pl.DeviceIdType.MESH
BF, F32 = jnp.bfloat16, jnp.float32
W = 1024
SH = 64
NJ = 4
NQ = 2
CW, RW = W // NJ, SH // NJ
ALL = slice(0, W)
X_FIRST = frozenset([(0, 1), (0, 3), (1, 1), (1, 3), (3, 1), (3, 2)])
UNIT_US = 22.3
HOP_US = {"z+": 2.3, "z-": 2.3, "y+": 2.3, "y-": 2.3, "x": 3.3, "dp": 1.1}
CORE = 1.0
NT = (((1,), (1,)), ((), ()))
TN = (((0,), (0,)), ((), ()))
ORDER = (
    7, 31, 71, 47, 55, 63, 39, 87, 72, 95, 0, 147, 64, 15, 77, 48, 23, 82, 24, 139, 32, 92, 1, 163,
    140, 40, 65, 49, 16, 93, 56, 25, 103, 132, 8, 33, 2, 141, 41, 17, 57, 100, 26, 156, 66, 133, 9, 50,
    4, 42, 94, 58, 34, 27, 28, 101, 157, 68, 3, 10, 52, 171, 18, 44, 67, 60, 43, 59, 51, 36, 29, 5,
    69, 12, 35, 11, 123, 164, 70, 102, 53, 20, 45, 6, 61, 73, 115, 37, 19, 155, 131, 75, 204, 54, 86, 30,
    90, 88, 207, 84, 165, 116, 13, 108, 38, 76, 74, 21, 46, 81, 79, 62, 89, 142, 158, 91, 99, 124, 117, 107,
    109, 148, 22, 83, 166, 85, 144, 14, 78, 134, 159, 80, 143, 205, 125, 160, 96, 149, 206, 118, 168, 110, 167, 136,
    145, 104, 135, 161, 150, 126, 120, 169, 97, 119, 112, 146, 179, 137, 111, 162, 195, 152, 105, 151, 127, 170, 203, 128,
    121, 176, 138, 98, 199, 113, 192, 129, 153, 200, 122, 183, 106, 177, 114, 175, 130, 212, 210, 214, 191, 154, 201, 187,
    180, 193, 208, 211, 215, 213, 172, 178, 196, 188, 209, 202, 184, 194, 181, 173, 197, 189, 185, 182, 174, 198, 190, 186,
)


class Task:
    def __init__(self, name, needs, groups, waits, cost, body, starts, rank):
        self.name, self.needs, self.groups, self.waits, self.cost = name, needs, groups, waits, cost
        self.body, self.starts, self.rank = body, starts, rank


def order_tasks(tasks, links, sizes):
    free, arrive, done, now = {}, {}, {}, 0.0
    left, result = list(tasks), []
    while left:
        best = None
        for task in left:
            if any(n not in done for n in task.needs) or any(w not in arrive for w in task.waits):
                continue
            ready = max([now] + [done[n] for n in task.needs] + [arrive[w] for w in task.waits])
            key = (ready, task.rank)
            if best is None or key < best[0]:
                best = (key, task)
        (ready, _), task = best
        now = ready + CORE * task.cost + 0.03 * len(task.starts)
        done[task.name] = now
        for copy in task.starts:
            link = links[copy]
            begin = max(now, free.get(link, 0.0))
            free[link] = begin + sizes[copy]
            arrive[copy] = free[link] + HOP_US[link]
        left.remove(task)
        result.append(task)
    return result, now


def kernel(
    q_hbm, k_hbm, v_hbm, y_hbm, r_hbm, m_hbm, c_hbm,
    qg_hbm, kg_hbm, vg_hbm, ig_hbm,
    qg_ref, kg_ref, vg_ref, cf, kb, qb, yb, vb, rb, mf, mh0, mh1, ch, ph0, part, full, rbuf, part2, rbuf2, arec, rc, gpart, gfull, gbuf, fix,
    ssem, rsem, lsem, osem,
):
    dp, row, col = lax.axis_index("dp"), lax.axis_index("row"), lax.axis_index("col")
    z, xh = col // 2, col % 2
    xl, y = row // 4, row % 4
    zp, zm, z2, xo = (z + 1) % 4, (z + 3) % 4, (z + 2) % 4, 1 - xh
    yp, ym, y2, lo = (y + 1) % 4, (y + 3) % 4, (y + 2) % 4, 1 - xl
    device = {
        "z+": (dp, row, zp * 2 + xh),
        "z-": (dp, row, zm * 2 + xh),
        "xh": (dp, row, z * 2 + xo),
        "y+": (dp, xl * 4 + yp, col),
        "y-": (dp, xl * 4 + ym, col),
        "xl": (dp, lo * 4 + y, col),
        "dp": (1 - dp, row, col),
    }

    loads = {}

    def load(name, src, dst):
        copy = pltpu.make_async_copy(src, dst, lsem.at[len(loads)])
        copy.start()
        loads[name] = copy

    def rows_of(g):
        return pl.ds(g * CW, CW)

    load("K1", k_hbm.at[0, 1], kb.at[1])
    for g in range(NJ):
        load(("C", g), c_hbm.at[rows_of(g)], cf.at[rows_of(g)])
    load("K0", k_hbm.at[0, 0], kb.at[0])
    for g in range(NJ):
        load(("M", g), m_hbm.at[rows_of(g)], mf.at[rows_of(g)])
    load("Y1", y_hbm.at[0, 1], yb.at[1])
    load("Q1", q_hbm.at[0, 1], qb.at[1])
    load("R", r_hbm, rb)
    load("V", v_hbm.at[0, :, col], vb)
    load("Y0", y_hbm.at[0, 0], yb.at[0])
    load("Q0", q_hbm.at[0, 0], qb.at[0])
    loaded = set()

    def need(*names):
        for name in names:
            if name not in loaded:
                loaded.add(name)
                loads[name].wait()

    barrier = pltpu.get_barrier_semaphore()
    for partner in device.values():
        pl.semaphore_signal(barrier, inc=1, device_id=partner, device_id_type=MESH)

    def rates():
        need("R")
        at = lax.broadcasted_iota(jnp.int32, (SH, 8 * SH), 1)
        own = lax.broadcasted_iota(jnp.int32, (SH, 8 * SH), 0) + col * SH
        for b in range(2):
            picked = jnp.where(at == own, jnp.broadcast_to(rb[0, b : b + 1, :], (SH, 8 * SH)), 0.0)
            rc[b] = jnp.broadcast_to(jnp.sum(picked, axis=1, keepdims=True), (SH, 128))

    copies, links, sizes, groups, sends = {}, {}, {}, {}, {}

    def waiter(ref, sem):
        return pltpu.make_async_copy(ref, ref, sem)

    def send_group(key, ref):
        sends[key] = waiter(ref, ssem.at[len(sends)]), ssem.at[len(sends)]

    def group(name, ref):
        groups[name] = waiter(ref, rsem.at[len(groups)]), rsem.at[len(groups)]

    def copy(name, link, src, dst, units, job, into=None):
        if into is None:
            group(name, dst)
            into = name
        copies[name] = pltpu.make_async_remote_copy(
            src_ref=src, dst_ref=dst, send_sem=sends[job][1], recv_sem=groups[into][1],
            device_id=device[link], device_id_type=MESH,
        )
        members.setdefault(into, []).append(name)
        links[name] = "x" if link in ("xh", "xl") else link
        sizes[name] = units * (UNIT_US if link != "dp" else 1.2)

    members = {}

    tasks = []

    def task(name, needs, waits, cost, body, starts, rank):
        tasks.append(Task(name, needs, waits, [c for w in waits for c in members[w]], cost, body, starts, rank))

    def out(i, ref, hbm, *index):
        pltpu.make_async_copy(ref.at[index], hbm.at[index], osem.at[i]).start()

    def f32(ref, *index):
        return ref[index].astype(F32)

    def finish(q, cs, rs, total):
        if "V" not in loaded:
            rates()
        need("V")
        b = 1 if q in (0, 3) else 0
        rate = jnp.broadcast_to(rc[b, rs, 0:1], total.shape)
        if q == 2:
            total = total + fix[0, rs, cs]
        if q == 3:
            total = 0.999 * total - fix[1, rs, cs]
        if q in (0, 2):
            scaled = (rate * total).astype(BF)
            vg_ref[0, b, rs, cs] = scaled
            out(2, vg_ref, vg_hbm, 0, b, rs, cs)
            full[q, z, xh, rs, cs] = -scaled
        else:
            full[q, z, xh, rs, cs] = (rate * (total - f32(vb, b, rs, cs))).astype(BF)

    def reduce_job(tag, q, rs, cs, rank, P4, R, first, pieces, names, after, after_cost, after_starts, more=()):
        ring, ahead, behind, far, mine, other = pieces
        up, down, side = names
        u = (rs.stop - rs.start) * (cs.stop - cs.start) / (SH * W) / 8.0

        def part_at(i, half):
            return P4(i, half)

        def slot(k):
            return R.at[q, k, rs, cs]

        n = lambda k: (tag, q, rank, k)
        job = (tag[0], q)
        if job not in sends:
            send_group(job, R.at[q])
        group(n("D1"), R.at[q, pl.ds(0, 2), rs, cs])
        group(n("A"), R.at[q, pl.ds(0, 3), rs, cs])
        group(n("B"), R.at[q, pl.ds(0, 2), rs, cs])
        copy(n("D1p"), up, part_at(far, mine), slot(0), u, job, n("D1"))
        copy(n("D1m"), down, part_at(far, other), slot(1), u, job, n("D1"))
        copy(n("D2pA"), up, part_at(ahead, mine), slot(2), u, job, n("A"))
        copy(n("D2pB"), up, part_at(ahead, other), slot(3), u, job, n("B"))
        copy(n("D2mA"), down, part_at(behind, mine), slot(4), u, job, n("A"))
        copy(n("D2mB"), down, part_at(behind, other), slot(5), u, job, n("B"))
        copy(n("DX"), side, part_at(ring, other), slot(6), u, job, n("A"))

        def add(ref, *slots):
            total = ref[...].astype(F32)
            for k in slots:
                total = total + R[q, k, rs, cs].astype(F32)
            return total

        def s1():
            ref = part_at(ahead, mine)
            ref[...] = add(ref, 0).astype(BF)
            ref = part_at(behind, other)
            ref[...] = add(ref, 1).astype(BF)

        def s2():
            ref = part_at(ring, other)
            ref[...] = add(ref, 3, 5).astype(BF)

        def s3():
            after(rs, cs, add(part_at(ring, mine), 2, 4, 6))

        vpu = u * 8 * 0.1 + 0.03
        task(n("s1"), [first], [n("D1")], 2 * vpu, s1, [n("D2pA"), n("D2mB")], rank)
        task(n("s2"), [n("s1")], [n("B")], vpu, s2, [n("DX")], rank)
        task(n("s3"), [n("s2")], [n("A")], vpu + after_cost, s3, after_starts, rank)
        tasks[-1].needs.extend(more)
        return [n("D1p"), n("D1m"), n("D2pB"), n("D2mA")], n("s3")

    def gather_job(tag, q, rs, cs, rank, F4, R, pieces, names):
        ring, ahead, behind, _, mine, other = pieces
        up, down, side = names
        u = (rs.stop - rs.start) * (cs.stop - cs.start) / (SH * W) / 8.0
        n = lambda k: (tag, q, rank, k)
        job = (tag[0], q)
        group(n("G"), R.at[q, pl.ds(0, 4), rs, cs])
        copy(n("GX"), side, F4(ring, mine), F4(ring, mine), u, job)
        copy(n("Gop"), up, F4(ring, mine), F4(ring, mine), u, job)
        copy(n("Gom"), down, F4(ring, mine), F4(ring, mine), u, job, n("G"))
        copy(n("Gtp"), up, F4(ring, other), F4(ring, other), u, job, n("G"))
        copy(n("Gtm"), down, F4(ring, other), F4(ring, other), u, job)
        copy(n("Fp"), up, F4(behind, mine), F4(behind, mine), u, job, n("G"))
        copy(n("Fm"), down, F4(ahead, other), F4(ahead, other), u, job, n("G"))

        def follow(last):
            task(n("s4"), [last], [n("GX")], 0.05, None, [n("Gtp"), n("Gtm")], rank)
            task(n("s5p"), [last], [n("Gop")], 0.05, None, [n("Fp")], rank)
            task(n("s5m"), [last], [n("Gtm")], 0.05, None, [n("Fm")], rank)
            task(n("end"), [n("s4"), n("s5p"), n("s5m")], [n("G")], 0.05, None, [], rank)
            return n("end")

        return [n("GX"), n("Gop"), n("Gom")], follow

    z_ring, z_names = (z, zp, zm, z2, xh, xo), ("z+", "z-", "xh")
    y_ring, y_names = (y, yp, ym, y2, xl, lo), ("y+", "y-", "xl")

    def col_sends(q):
        if ("c", q) not in sends:
            send_group(("c", q), rbuf.at[pl.ds(0, 2)])

    def col_z(q, rs, cs, rank, first, more):
        def P4(i, half):
            return part.at[q, i, half, rs, cs]

        def F4(i, half):
            return full.at[q, i, half, rs, cs]

        col_sends(q)
        begin, follow = gather_job("cz", q, rs, cs, rank, F4, rbuf, z_ring, z_names)
        starts, last = reduce_job(
            "cz", q, rs, cs, rank, P4, rbuf, first, z_ring, z_names,
            lambda rs, cs, total: finish(q, cs, rs, total), 0.1, begin, more,
        )
        return starts, follow(last)

    def keys_job(rank, first):
        rs, cs = slice(0, SH), slice(0, 128)

        def P4(i, half):
            return gpart.at[i, half]

        def F4(i, half):
            return gfull.at[half, i]

        def store(rs, cs, total):
            gfull[xl, y] = total.astype(BF)

        send_group(("k", 0), rbuf.at[pl.ds(0, 2), :, rs, cs])
        begin, follow = gather_job("kk", 0, rs, cs, rank, F4, gbuf, y_ring, y_names)
        starts, last = reduce_job("kk", 0, rs, cs, rank, P4, gbuf, first, z_ring, z_names, store, 0.0, begin)
        return starts, follow(last)

    def col_x(q, rs, cs, rank, first, more):
        u = (rs.stop - rs.start) * (cs.stop - cs.start) / (SH * W) / 8.0
        half = (cs.stop - cs.start) // 2
        cl, cr = slice(cs.start, cs.start + half), slice(cs.start + half, cs.stop)
        n = lambda k: ("cx", q, rank, k)

        def P3(i, c):
            return part.at[q, i, xh, rs, c]

        def F3(i, c):
            return full.at[q, i, xh, rs, c]

        def slot(k, c):
            return rbuf.at[q, k, rs, c]

        job = ("c", q)
        col_sends(q)
        group(n("D1"), slot(4, cs))
        group(n("D2"), rbuf.at[q, pl.ds(0, 2), rs, cs])
        group(n("F"), slot(4, cs))
        group(n("X"), rbuf.at[q, pl.ds(0, 4), rs, cs])
        copy(n("DX"), "xh", part.at[q, :, xo, rs, cs], rbuf.at[q, pl.ds(0, 4), rs, cs], 4 * u, job)
        copy(n("D1p"), "z+", P3(z2, cl), slot(4, cl), u / 2, job, n("D1"))
        copy(n("D1m"), "z-", P3(z2, cr), slot(4, cr), u / 2, job, n("D1"))
        copy(n("D2pL"), "z+", P3(zp, cl), slot(5, cl), u / 2, job, n("D2"))
        copy(n("D2pR"), "z+", P3(zp, cr), slot(5, cr), u / 2, job, n("D2"))
        copy(n("D2mL"), "z-", P3(zm, cl), slot(6, cl), u / 2, job, n("D2"))
        copy(n("D2mR"), "z-", P3(zm, cr), slot(6, cr), u / 2, job, n("D2"))
        copy(n("Gp"), "z+", F3(z, cs), F3(z, cs), u, job)
        copy(n("Gm"), "z-", F3(z, cs), F3(z, cs), u, job)
        copy(n("Fp"), "z+", F3(zm, cl), F3(zm, cl), u / 2, job, n("F"))
        copy(n("Fm"), "z-", F3(zp, cr), F3(zp, cr), u / 2, job, n("F"))
        copy(n("X0"), "xh", F3(z, cs), F3(z, cs), u, job, n("X"))
        copy(n("Xm"), "xh", F3(zm, cs), F3(zm, cs), u, job, n("X"))
        copy(n("Xp"), "xh", F3(zp, cs), F3(zp, cs), u, job, n("X"))
        copy(n("X2"), "xh", F3(z2, cs), F3(z2, cs), u, job, n("X"))

        def s1():
            for i in range(4):
                part[q, i, xh, rs, cs] = (f32(part, q, i, xh, rs, cs) + f32(rbuf, q, i, rs, cs)).astype(BF)

        def s2():
            part[q, zp, xh, rs, cl] = (f32(part, q, zp, xh, rs, cl) + f32(rbuf, q, 4, rs, cl)).astype(BF)
            part[q, zm, xh, rs, cr] = (f32(part, q, zm, xh, rs, cr) + f32(rbuf, q, 4, rs, cr)).astype(BF)

        def s3():
            finish(q, cs, rs, f32(part, q, z, xh, rs, cs) + f32(rbuf, q, 5, rs, cs) + f32(rbuf, q, 6, rs, cs))

        vpu = u * 8 * 0.1 + 0.03
        task(n("s1"), [first], [n("DX")], 2 * vpu, s1, [n("D1p"), n("D1m"), n("D2pR"), n("D2mL")], rank)
        task(n("s2"), [n("s1")], [n("D1")], 2 * vpu, s2, [n("D2pL"), n("D2mR")], rank)
        task(n("s3"), [n("s2"), *more], [n("D2")], vpu + 0.1, s3, [n("Gp"), n("Gm"), n("X0")], rank)
        task(n("s4p"), [n("s3")], [n("Gp")], 0.05, None, [n("Fp"), n("Xm")], rank)
        task(n("s4m"), [n("s3")], [n("Gm")], 0.05, None, [n("Fm"), n("Xp")], rank)
        task(n("s5"), [n("s4p"), n("s4m")], [n("F")], 0.05, None, [n("X2")], rank)
        task(n("end"), [n("s5")], [n("X")], 0.05, None, [], rank)
        return [n("DX")], n("end")

    def row_job(u, rs, cs, rank, first):
        def P4(i, half):
            return part2.at[u, half, i, rs, cs]

        def store(rs, cs, total):
            i, b = u // 2, u % 2
            ref, hbm = ((qg_ref, qg_hbm), (kg_ref, kg_hbm))[i]
            ref[0, b, rs, cs] = total.astype(BF)
            out(i, ref, hbm, 0, b, rs, cs)

        return reduce_job(
            "r", u, rs, cs, rank, P4, rbuf2, first, y_ring, y_names, store, 0.0, [],
        )

    def dot(a, b, dims=None):
        if dims is None:
            return jnp.dot(a, b, preferred_element_type=F32)
        return lax.dot_general(a, b, dims, preferred_element_type=F32)

    def whole(ref, *index):
        return ref[index].reshape(8 * SH, -1)

    def some(ref, *index):
        return ref[index].reshape(8 * RW, W)

    ends = [[None] * NJ for _ in range(4)]
    everything = slice(0, SH)
    full_cols = slice(0, W)

    def cols(g):
        return slice(g * CW, (g + 1) * CW)

    def toks(k):
        return slice(k * RW, (k + 1) * RW)

    def spread(q, block, width, value, rs, cs):
        part[q, :, :, rs, cs] = value.astype(BF).reshape(4, 2, rs.stop - rs.start, cs.stop - cs.start)

    def phase_a(q, g, rank):
        b, src, half = (1, cf, ch) if q == 0 else (0, mf, mh0)
        rs, cs = everything, cols(g)
        name = ("P", q, g)

        def body():
            need("K1" if q == 0 else "K0", ("C" if q == 0 else "M", g))
            half[cs, :] = src[cs, :].astype(BF)
            spread(q, g, CW, dot(whole(kb, b), half[cs, :], NT), rs, cs)

        make = col_x if (q, g) in X_FIRST else col_z
        starts, ends[q][g] = make(q, rs, cs, rank, name, [])
        task(name, [], [], 0.35, body, starts, rank)

    for i, (q, g) in enumerate([(0, g) for g in range(NJ)] + [(1, g) for g in range(NJ)]):
        phase_a(q, g, i)

    def keys_product():
        name = ("KK",)

        def body():
            need("K0", "K1")
            odd = y % 2
            rhs = kb[odd, pl.ds(2 * (row // 2), 2)].reshape(128, W)
            value = dot(kb[1 - odd].reshape(8 * SH, W), rhs, NT)
            gpart[...] = value.astype(BF).reshape(4, 2, SH, 128)

        starts, end = keys_job(7.2, name)
        task(name, [], [], 0.4, body, starts, 7.2)
        return end

    keys_end = keys_product()

    def correction(q, g):
        cs = cols(g)
        src, odd = (0, 1) if q == 2 else (1, 0)

        def body():
            lhs = jnp.concatenate([gfull[r // 4, r % 4] for r in range(odd, 8, 2)], axis=1)
            fix[q - 2, :, cs] = dot(lhs, full[src, :, :, :, cs].reshape(8 * SH, CW))

        task(("FX", q, g), [keys_end, ends[src][g]], [], 0.08, body, [], 7.4 if q == 2 else 8.4)

    def project_known(g):
        cs = cols(g)

        def body():
            need("Y1", "Q1")
            step = dot(yb[1, :, :, cs].reshape(8 * SH, CW), whole(qb, 1), TN)
            before = cf[cs, :]
            cf[cs, :] = 0.999 * before + step
            ph0[cs, :] = (1.899 * before + step).astype(BF)

        task(("PK", g), [("P", 0, g)], [], 0.35, body, [], 7.1)

    def project_update(g):
        cs = cols(g)

        def body():
            step = dot(full[0, :, :, :, cs].reshape(8 * SH, CW), whole(kb, 1), TN)
            adjoint = cf[cs, :] + step
            cf[cs, :] = adjoint
            ph0[cs, :] = (adjoint + 0.9 * ch[cs, :].astype(F32)).astype(BF)

        task(("PU", g), [ends[0][g]] + [("P", 2, k) for k in range(NJ)], [], 0.45, body, [], 16.1)

    def memory_update(g):
        cs = cols(g)

        def body():
            need("K0")
            step = dot(full[1, :, :, :, cs].reshape(8 * SH, CW), whole(kb, 0), TN)
            mh1[cs, :] = (0.999 * mf[cs, :] - step).astype(BF)

        task(("MU", g), [ends[1][g]], [], 0.38, body, [], 16.2)

    for g in range(NJ):
        project_known(g)
        correction(2, g)
        correction(3, g)
        project_update(g)
        memory_update(g)
    all_pu = [("PU", g) for g in range(NJ)]
    all_mu = [("MU", g) for g in range(NJ)]

    def query_part(u, g, rank):
        mem = mh0 if u == 0 else mh1
        rs, cs = everything, slice(g * W // NQ, (g + 1) * W // NQ)
        name = ("QP", u, g)

        def body():
            need("Y%d" % u)
            for lo in range(cs.start, cs.stop, CW):
                value = dot(whole(yb, u), mem[:, lo : lo + CW])
                part2[u, :, :, rs, lo : lo + CW] = value.astype(BF).reshape(2, 4, SH, CW)

        starts, _ = row_job(u, rs, cs, rank, name)
        deps = [("P", 1, g) for g in range(NJ)] if u == 0 else all_mu
        task(name, deps, [], 0.6, body, starts, rank)

    for g in range(NQ):
        query_part(0, g, 20 + g)
        query_part(1, g, 24 + g)

    def phase_b(q, k, rank):
        b, half = (0, ph0) if q == 2 else (1, mh0)
        deps = [("PK", g) if q == 2 else ("P", 1, g) for g in range(NJ)]
        rs, cs = toks(k), full_cols
        name = ("P", q, k)

        def body():
            need("K%d" % b)
            lhs = some(kb, b, slice(None), rs)
            for n in range(NJ):
                spread(q, n, CW, dot(lhs, half[cols(n), :], NT), rs, cols(n))

        make = col_x if (q, k) in X_FIRST else col_z
        starts, ends[q][k] = make(q, rs, cs, rank, name, [("FX", q, g) for g in range(NJ)])
        task(name, deps, [], 0.7, body, starts, rank)

    for i, (q, k) in enumerate([(2, k) for k in range(NJ)] + [(3, k) for k in range(NJ)]):
        phase_b(q, k, 8 + i)

    def key_part(u, k, rank):
        rs = toks(k)
        f, w, mem, proj = (2, 1, mh0, ph0) if u == 2 else (0, 3, mh1, ch)
        name = ("KP", u, k)

        def body():
            err, wgt = some(full, f, slice(None), slice(None), rs), some(full, w, slice(None), slice(None), rs)
            for n in range(NJ):
                value = dot(err, mem[:, cols(n)]) - dot(wgt, proj[:, cols(n)])
                part2[u, :, :, rs, cols(n)] = value.astype(BF).reshape(2, 4, RW, CW)

        starts, _ = row_job(u, rs, full_cols, rank, name)
        deps = [ends[2][k]] + all_pu + all_mu if u == 2 else [ends[3][k]] + all_pu + all_mu
        task(name, deps, [], 0.65, body, starts, rank)

    for k in range(NJ):
        key_part(2, k, 17 + k / 10)
        key_part(3, k, 18 + k / 10)

    def adjoint_early(g):
        cs = cols(g)

        def body():
            need("Y0", "Q0")
            cf[cs, :] = 0.999 * cf[cs, :] + dot(yb[0, :, :, cs].reshape(8 * SH, CW), whole(qb, 0), TN)

        task(("AE", g), [("PU", g)], [], 0.38, body, [], 30)

    def adjoint_late(g):
        cs = cols(g)

        def body():
            step = dot(full[2, :, :, :, cs].reshape(8 * SH, CW), whole(kb, 0), TN)
            qb[g // 2, four] = (cf[cs, :] + step).astype(BF).reshape(4, SH, W)

        four = slice(g % 2 * 4, g % 2 * 4 + 4)
        copy(("A", g), "dp", qb.at[g // 2, four], arec.at[g // 2, four], 0.5, "A")
        task(("AL", g), [("AE", h) for h in range(NJ)] + ends[2], [], 0.38, body, [("A", g)], 19)

        def total():
            cf[cs, :] = (qb[g // 2, four].astype(F32) + arec[g // 2, four].astype(F32)).reshape(CW, W)
            out(3, cf, ig_hbm, cs)

        task(("AT", g), [("AL", g)], [("A", g)], 0.1, total, [], 31)

    for g in range(NJ):
        adjoint_early(g)
    send_group("A", arec)
    for g in range(NJ):
        adjoint_late(g)

    order, _ = order_tasks(tasks, links, sizes)
    if ORDER:
        order = [tasks[i] for i in ORDER]
    held = []
    for item in order:
        if held is not None and (item.groups or len(held) == 6):
            pl.semaphore_wait(barrier, len(device))
            for name in [name for early in held for name in early.starts]:
                copies[name].start()
            held = None
        for name in item.groups:
            groups[name][0].wait()
        if item.body is not None:
            item.body()
        if held is not None:
            held.append(item)
            continue
        for name in item.starts:
            copies[name].start()
    for wait, _ in sends.values():
        wait.wait()
    for i, (ref, hbm) in enumerate(((qg_ref, qg_hbm), (kg_ref, kg_hbm), (vg_ref, vg_hbm), (cf, ig_hbm))):
        pltpu.make_async_copy(ref, hbm, osem.at[i]).wait()


def on_device(query, key, value, out_grad, rate, memory_init, memory_cot):
    shared = (1, 2, 8, SH, W)
    vm = pltpu.VMEM
    n_recv, n_send = 17 * 7 + (2 * NQ + 8) * 3 + NJ, 10
    outs = pl.pallas_call(
        kernel,
        out_shape=(
            jax.ShapeDtypeStruct((1, 2, SH, W), BF),
            jax.ShapeDtypeStruct((1, 2, SH, W), BF),
            jax.ShapeDtypeStruct((1, 2, SH, W), BF),
            jax.ShapeDtypeStruct((W, W), F32),
        ),
        in_specs=[pl.BlockSpec(memory_space=pltpu.HBM)] * 7,
        out_specs=(pl.BlockSpec(memory_space=pl.ANY),) * 4,
        scratch_shapes=[
            vm((1, 2, SH, W), BF),
            vm((1, 2, SH, W), BF),
            vm((1, 2, SH, W), BF),
            vm((W, W), F32),
            vm((2, 8, SH, W), BF),
            vm((2, 8, SH, W), BF),
            vm((2, 8, SH, W), BF),
            vm((2, SH, W), BF),
            vm((1, 2, 8 * SH), F32),
            vm((W, W), F32),
            vm((W, W), BF),
            vm((W, W), BF),
            vm((W, W), BF),
            vm((W, W), BF),
            vm((4, 4, 2, SH, W), BF),
            vm((4, 4, 2, SH, W), BF),
            vm((4, 7, SH, W), BF),
            vm((4, 2, 4, SH, W), BF),
            vm((4, 7, SH, W), BF),
            vm((2, 8, SH, W), BF),
            vm((2, SH, 128), F32),
            vm((4, 2, SH, 128), BF),
            vm((2, 4, SH, 128), BF),
            vm((1, 7, SH, 128), BF),
            vm((2, SH, W), F32),
            pltpu.SemaphoreType.DMA((n_send,)),
            pltpu.SemaphoreType.DMA((n_recv,)),
            pltpu.SemaphoreType.DMA((16,)),
            pltpu.SemaphoreType.DMA((4,)),
        ],
        compiler_params=pltpu.CompilerParams(
            collective_id=0, has_side_effects=True, vmem_limit_bytes=56 * 2**20
        ),
        name="memory_backward",
    )(
        query.reshape(shared), key.reshape(shared), value.reshape(shared), out_grad.reshape(shared), rate,
        memory_init, memory_cot,
    )
    return publish(*outs)


def publish_kernel(*refs):
    ins, outs, held, (rsem, wsem) = refs[:4], refs[4:8], refs[8:12], refs[12:]
    whole = [(ins[i], held[i], outs[i]) for i in range(3)]
    rows = [pl.ds(g * 128, 128) for g in range(8)]
    parts = [(ins[3].at[r], held[3].at[r], outs[3].at[r]) for r in rows] + whole
    reads = [pltpu.make_async_copy(a, b, rsem.at[i]) for i, (a, b, _) in enumerate(parts)]
    writes = [pltpu.make_async_copy(b, c, wsem.at[i]) for i, (_, b, c) in enumerate(parts)]
    for read in reads:
        read.start()
    for read, write in zip(reads, writes):
        read.wait()
        write.start()
    for write in writes:
        write.wait()


def publish(*arrays):
    shapes = tuple(jax.ShapeDtypeStruct(a.shape, a.dtype) for a in arrays)
    return pl.pallas_call(
        publish_kernel,
        out_shape=shapes,
        in_specs=[pl.BlockSpec(memory_space=pl.ANY)] * 4,
        out_specs=(pl.BlockSpec(memory_space=pl.ANY),) * 4,
        scratch_shapes=[pltpu.VMEM(a.shape, a.dtype) for a in arrays]
        + [pltpu.SemaphoreType.DMA((11,)), pltpu.SemaphoreType.DMA((11,))],
        compiler_params=pltpu.CompilerParams(vmem_limit_bytes=60 * 2**20),
        name="publish",
    )(*arrays)


def solution(mesh):
    placed = (
        P("dp", None, None, "col"),
        P("dp", None, None, "col"),
        P("dp", None, None, "row"),
        P("dp", None, None, "row"),
        P("dp", None, None),
        P("row", "col"),
        P("row", "col"),
    )
    return jax.shard_map(
        on_device,
        mesh=mesh,
        in_specs=placed,
        out_specs=(
            P("dp", None, "row", "col"),
            P("dp", None, "row", "col"),
            P("dp", None, "col", "row"),
            P("row", "col"),
        ),
        check_vma=False,
    )
```

time: 128 us -> 91.1 us (0.71)
  Pallas kernels: 118 us -> 90.2 us
  local copies, waits for them, and re-layouts: 9.79 us -> 0 us
    pallas_call x1, Pallas kernels: 118 us -> 85.8 us  [on_device(): pl.pallas_call(kernel, out_shape=(jax.ShapeDtypeStruct((1, 2, SH, W), BF)...]
    unnamed x4 -> x0, local copies, waits for them, and re-layouts: 9.79 us -> none
    pallas_call x0 -> x1, Pallas kernels: none -> 4.35 us  [publish(): pl.pallas_call(publish_kernel, out_shape=shapes, in_specs=[pl.BlockSpec(m...]
where the time goes in v2:
time: 91.1 us; the launch traced here: 91 us
  Pallas kernels  90.2 us (99%)
    pallas_call x1, Pallas kernels, on_device(): pl.pallas_call(kernel, out_shape=(jax.ShapeDtypeStruct((1, 2, SH, W), BF)...  85.8 us
    pallas_call x1, Pallas kernels, publish(): pl.pallas_call(publish_kernel, out_shape=shapes, in_specs=[pl.BlockSpec(m...  4.35 us

profile of v2, /device:TPU:0, one launch (start us, length us, event | category | flops | bytes accessed | tf_op | source)
XLA Modules:
  0.0 91.0 jit_solution(881291080956071685)
XLA Ops:
  0.6 85.8 %memory_backward.1 = (bf16[1,2,64,1024]{3,2,1,0:T(8,128)(2,1)}, bf16[1,2,64,1024]{3,2,1,0:T(8,128)(2,1)}, bf16[1,2,64,1024]{3,2,1,0:T(8,128)(2,1)}, f32[1024,1024]{1,0:T(8,128)}) custom-call(bf16[1,2,8,64,1024]{4,3,2,1,0:T(8,128)(2,1)} %bitcast.4, bf16[1,2,8,64,1024]{4,3,2,1,0:T(8,128)(2,1)} %bitcast.5, bf16[1,2,8,64,1024]{4,3,2,1,0:T(8,128)(2,1)} %bitcast.6, ...), custom_call_target="tpu_custom_call" | custom-call | tf_op jit(solution)/shard_map/memory_backward/pallas_call | solution.py:599
  86.5 4.4 %publish.1 = (bf16[1,2,64,1024]{3,2,1,0:T(8,128)(2,1)}, bf16[1,2,64,1024]{3,2,1,0:T(8,128)(2,1)}, bf16[1,2,64,1024]{3,2,1,0:T(8,128)(2,1)}, f32[1024,1024]{1,0:T(8,128)}) custom-call(bf16[1,2,64,1024]{3,2,1,0:T(8,128)(2,1)} %get-tuple-element.8.refs_0_, bf16[1,2,64,1024]{3,2,1,0:T(8,128)(2,1)} %get-tuple-element.9.refs_1_, ...), custom_call_target="tpu_custom_call" | custom-call | tf_op jit(solution)/shard_map/publish/pallas_call | solution.py:669

commit v3 on v2

--- a/solution.py
+++ b/solution.py
@@ -15,22 +15,24 @@
 NQ = 2
 CW, RW = W // NJ, SH // NJ
 ALL = slice(0, W)
-X_FIRST = frozenset([(0, 1), (0, 3), (1, 1), (1, 3), (3, 1), (3, 2)])
-UNIT_US = 22.3
-HOP_US = {"z+": 2.3, "z-": 2.3, "y+": 2.3, "y-": 2.3, "x": 3.3, "dp": 1.1}
+X_FIRST = frozenset([(0, 0), (0, 3), (1, 0), (1, 1), (1, 2), (2, 3)])
+ROW_X_FIRST = frozenset([(2, 3), (3, 3)])
+UNIT_US = 23.4
+HOP_US = {"z+": 2.7, "z-": 2.7, "y+": 2.7, "y-": 2.7, "x": 3.7, "dp": 1.1}
 CORE = 1.0
 NT = (((1,), (1,)), ((), ()))
 TN = (((0,), (0,)), ((), ()))
 ORDER = (
-    7, 31, 71, 47, 55, 63, 39, 87, 72, 95, 0, 147, 64, 15, 77, 48, 23, 82, 24, 139, 32, 92, 1, 163,
-    140, 40, 65, 49, 16, 93, 56, 25, 103, 132, 8, 33, 2, 141, 41, 17, 57, 100, 26, 156, 66, 133, 9, 50,
-    4, 42, 94, 58, 34, 27, 28, 101, 157, 68, 3, 10, 52, 171, 18, 44, 67, 60, 43, 59, 51, 36, 29, 5,
-    69, 12, 35, 11, 123, 164, 70, 102, 53, 20, 45, 6, 61, 73, 115, 37, 19, 155, 131, 75, 204, 54, 86, 30,
-    90, 88, 207, 84, 165, 116, 13, 108, 38, 76, 74, 21, 46, 81, 79, 62, 89, 142, 158, 91, 99, 124, 117, 107,
-    109, 148, 22, 83, 166, 85, 144, 14, 78, 134, 159, 80, 143, 205, 125, 160, 96, 149, 206, 118, 168, 110, 167, 136,
-    145, 104, 135, 161, 150, 126, 120, 169, 97, 119, 112, 146, 179, 137, 111, 162, 195, 152, 105, 151, 127, 170, 203, 128,
-    121, 176, 138, 98, 199, 113, 192, 129, 153, 200, 122, 183, 106, 177, 114, 175, 130, 212, 210, 214, 191, 154, 201, 187,
-    180, 193, 208, 211, 215, 213, 172, 178, 196, 188, 209, 202, 184, 194, 181, 173, 197, 189, 185, 182, 174, 198, 190, 186,
+    15, 7, 68, 23, 31, 63, 39, 47, 55, 104, 174, 69, 166, 64, 79, 0, 8, 16, 84, 56, 24, 74, 134, 1,
+    9, 32, 118, 17, 142, 25, 40, 126, 96, 57, 33, 2, 48, 127, 26, 92, 18, 65, 41, 10, 34, 49, 3, 111,
+    4, 28, 135, 100, 27, 19, 42, 11, 58, 36, 50, 35, 12, 66, 119, 128, 20, 21, 29, 5, 112, 44, 13, 43,
+    159, 158, 37, 120, 136, 51, 52, 150, 22, 67, 167, 80, 45, 6, 30, 85, 82, 14, 75, 59, 70, 129, 87, 60,
+    151, 97, 113, 53, 160, 38, 143, 168, 71, 61, 73, 137, 72, 101, 152, 130, 46, 121, 114, 210, 76, 144, 93, 131,
+    54, 81, 62, 86, 161, 169, 139, 108, 132, 89, 83, 138, 115, 78, 153, 122, 116, 145, 98, 77, 102, 123, 133, 162,
+    163, 88, 170, 194, 105, 171, 124, 140, 154, 117, 178, 155, 94, 146, 207, 164, 172, 147, 191, 90, 125, 186, 106, 156,
+    141, 202, 175, 148, 165, 198, 208, 103, 95, 173, 206, 183, 157, 190, 149, 182, 107, 209, 211, 213, 195, 215, 187, 176,
+    212, 109, 179, 184, 99, 192, 199, 203, 196, 188, 180, 200, 217, 204, 177, 216, 185, 189, 214, 218, 110, 91, 197, 201,
+    193, 205, 181,
 )
 
 
@@ -68,7 +70,7 @@
 def kernel(
     q_hbm, k_hbm, v_hbm, y_hbm, r_hbm, m_hbm, c_hbm,
     qg_hbm, kg_hbm, vg_hbm, ig_hbm,
-    qg_ref, kg_ref, vg_ref, cf, kb, qb, yb, vb, rb, mf, mh0, mh1, ch, ph0, part, full, rbuf, part2, rbuf2, arec, rc, gpart, gfull, gbuf, fix,
+    qg_ref, kg_ref, vg_ref, cf, kb, qb, yb, vb, rb, mf, mh0, mh1, ch, ph0, part, full, rbuf, part2, rbuf2, arec, rc, gpart, gfull, gbuf, fix, upart, ufull, ubuf, q1,
     ssem, rsem, lsem, osem,
 ):
     dp, row, col = lax.axis_index("dp"), lax.axis_index("row"), lax.axis_index("col")
@@ -83,15 +85,15 @@
         "y+": (dp, xl * 4 + yp, col),
         "y-": (dp, xl * 4 + ym, col),
         "xl": (dp, lo * 4 + y, col),
+        "y2": (dp, xl * 4 + y2, col),
+        "z2": (dp, row, z2 * 2 + xh),
         "dp": (1 - dp, row, col),
     }
 
     loads = {}
 
     def load(name, src, dst):
-        copy = pltpu.make_async_copy(src, dst, lsem.at[len(loads)])
-        copy.start()
-        loads[name] = copy
+        loads[name] = pltpu.make_async_copy(src, dst, lsem.at[len(loads)])
 
     def rows_of(g):
         return pl.ds(g * CW, CW)
@@ -109,12 +111,28 @@
     load("Y0", y_hbm.at[0, 0], yb.at[0])
     load("Q0", q_hbm.at[0, 0], qb.at[0])
     loaded = set()
+    stages = [
+        ["K1"] + [("C", g) for g in range(NJ)],
+        ["K0"] + [("M", g) for g in range(NJ)],
+        ["Y1", "Q1", "R", "V", "Y0", "Q0"],
+    ]
+
+    def next_stage():
+        for name in stages.pop(0):
+            loads[name].start()
 
     def need(*names):
         for name in names:
-            if name not in loaded:
-                loaded.add(name)
-                loads[name].wait()
+            if name in loaded:
+                continue
+            while any(name in stage for stage in stages):
+                next_stage()
+            loads[name].wait()
+            loaded.add(name)
+            if stages and name in (("C", 0), ("M", 0)):
+                next_stage()
+
+    next_stage()
 
     barrier = pltpu.get_barrier_semaphore()
     for partner in device.values():
@@ -139,7 +157,7 @@
     def group(name, ref):
         groups[name] = waiter(ref, rsem.at[len(groups)]), rsem.at[len(groups)]
 
-    def copy(name, link, src, dst, units, job, into=None):
+    def copy(name, link, src, dst, units, job, into=None, over=None):
         if into is None:
             group(name, dst)
             into = name
@@ -148,7 +166,7 @@
             device_id=device[link], device_id_type=MESH,
         )
         members.setdefault(into, []).append(name)
-        links[name] = "x" if link in ("xh", "xl") else link
+        links[name] = over or ("x" if link in ("xh", "xl") else link)
         sizes[name] = units * (UNIT_US if link != "dp" else 1.2)
 
     members = {}
@@ -283,19 +301,35 @@
     def keys_job(rank, first):
         rs, cs = slice(0, SH), slice(0, 128)
 
-        def P4(i, half):
-            return gpart.at[i, half]
-
-        def F4(i, half):
-            return gfull.at[half, i]
-
-        def store(rs, cs, total):
-            gfull[xl, y] = total.astype(BF)
-
-        send_group(("k", 0), rbuf.at[pl.ds(0, 2), :, rs, cs])
-        begin, follow = gather_job("kk", 0, rs, cs, rank, F4, gbuf, y_ring, y_names)
-        starts, last = reduce_job("kk", 0, rs, cs, rank, P4, gbuf, first, z_ring, z_names, store, 0.0, begin)
-        return starts, follow(last)
+        n = lambda k: ("kk", 0, rank, k)
+        u, job = 1 / 64, ("k", 0)
+        send_group(job, rbuf.at[pl.ds(0, 2), :, rs, cs])
+        group(n("Z"), gbuf.at[0, pl.ds(0, 6)])
+        group(n("Y"), gbuf.at[0, pl.ds(0, 6)])
+        for i, (there, at, cost) in enumerate((("z+", zp, 1), ("z-", zm, 1), ("z2", z2, 2))):
+            over = "z+" if i == 2 else there
+            copy(n(there), there, gpart.at[at], gbuf.at[0, pl.ds(2 * i, 2)], 2 * cost * u, job, n("Z"), over)
+        copy(n("DX"), "xh", gpart.at[z, xo], gbuf.at[0, 6], u, job)
+        copy(n("GX"), "xl", gfull.at[xl, y], gfull.at[xl, y], u, job)
+        for there, cost in (("y+", 1), ("y-", 1), ("y2", 2)):
+            over = "y+" if there == "y2" else there
+            copy(n(there), there, gfull.at[:, y], gfull.at[:, y], 2 * cost * u, job, n("Y"), over)
+
+        def s1():
+            for half in (xo, xh):
+                total = gpart[z, half].astype(F32)
+                for i in range(3):
+                    total = total + gbuf[0, 2 * i + half].astype(F32)
+                gpart[z, half] = total.astype(BF)
+
+        def s2():
+            gfull[xl, y] = (gpart[z, xh].astype(F32) + gbuf[0, 6].astype(F32)).astype(BF)
+
+        task(n("s1"), [first], [n("Z")], 0.1, s1, [n("DX")], rank)
+        task(n("s2"), [n("s1")], [n("DX")], 0.06, s2, [n("GX")], rank)
+        task(n("s3"), [n("s2")], [n("GX")], 0.06, None, [n("y+"), n("y-"), n("y2")], rank)
+        task(n("end"), [n("s3")], [n("Y")], 0.06, None, [], rank)
+        return [n("z+"), n("z-"), n("z2")], n("end")
 
     def col_x(q, rs, cs, rank, first, more):
         u = (rs.stop - rs.start) * (cs.stop - cs.start) / (SH * W) / 8.0
@@ -360,6 +394,9 @@
             return part2.at[u, half, i, rs, cs]
 
         def store(rs, cs, total):
+            if u == 1:
+                q1[rs, cs] = total
+                return
             i, b = u // 2, u % 2
             ref, hbm = ((qg_ref, qg_hbm), (kg_ref, kg_hbm))[i]
             ref[0, b, rs, cs] = total.astype(BF)
@@ -368,6 +405,44 @@
         return reduce_job(
             "r", u, rs, cs, rank, P4, rbuf2, first, y_ring, y_names, store, 0.0, [],
         )
+
+    def row_x(u, rs, cs, rank, first):
+        share = (rs.stop - rs.start) * (cs.stop - cs.start) / (SH * W) / 8.0
+        half = (cs.stop - cs.start) // 2
+        cl, cr = slice(cs.start, cs.start + half), slice(cs.start + half, cs.stop)
+        n = lambda k: ("rx", u, rank, k)
+        job = ("r", u)
+        if job not in sends:
+            send_group(job, rbuf2.at[u])
+        P3 = lambda i, c: part2.at[u, xl, i, rs, c]
+        slot = lambda k, c: rbuf2.at[u, k, rs, c]
+        group(n("D1"), slot(4, cs))
+        group(n("D2"), rbuf2.at[u, pl.ds(0, 2), rs, cs])
+        copy(n("DX"), "xl", part2.at[u, lo, :, rs, cs], rbuf2.at[u, pl.ds(0, 4), rs, cs], 4 * share, job)
+        copy(n("D1p"), "y+", P3(y2, cl), slot(4, cl), share / 2, job, n("D1"))
+        copy(n("D1m"), "y-", P3(y2, cr), slot(4, cr), share / 2, job, n("D1"))
+        copy(n("D2pL"), "y+", P3(yp, cl), slot(5, cl), share / 2, job, n("D2"))
+        copy(n("D2pR"), "y+", P3(yp, cr), slot(5, cr), share / 2, job, n("D2"))
+        copy(n("D2mL"), "y-", P3(ym, cl), slot(6, cl), share / 2, job, n("D2"))
+        copy(n("D2mR"), "y-", P3(ym, cr), slot(6, cr), share / 2, job, n("D2"))
+
+        def s1():
+            for i in range(4):
+                part2[u, xl, i, rs, cs] = (f32(part2, u, xl, i, rs, cs) + f32(rbuf2, u, i, rs, cs)).astype(BF)
+
+        def s2():
+            part2[u, xl, yp, rs, cl] = (f32(part2, u, xl, yp, rs, cl) + f32(rbuf2, u, 4, rs, cl)).astype(BF)
+            part2[u, xl, ym, rs, cr] = (f32(part2, u, xl, ym, rs, cr) + f32(rbuf2, u, 4, rs, cr)).astype(BF)
+
+        def s3():
+            total = f32(part2, u, xl, y, rs, cs) + f32(rbuf2, u, 5, rs, cs) + f32(rbuf2, u, 6, rs, cs)
+            kg_ref[0, u - 2, rs, cs] = total.astype(BF)
+            out(1, kg_ref, kg_hbm, 0, u - 2, rs, cs)
+
+        task(n("s1"), [first], [n("DX")], 0.1, s1, [n("D1p"), n("D1m"), n("D2pR"), n("D2mL")], rank)
+        task(n("s2"), [n("s1")], [n("D1")], 0.06, s2, [n("D2pL"), n("D2mR")], rank)
+        task(n("s3"), [n("s2")], [n("D2")], 0.06, s3, [], rank)
+        return [n("DX")], n("s3")
 
     def dot(a, b, dims=None):
         if dims is None:
@@ -479,23 +554,57 @@
     all_mu = [("MU", g) for g in range(NJ)]
 
     def query_part(u, g, rank):
-        mem = mh0 if u == 0 else mh1
         rs, cs = everything, slice(g * W // NQ, (g + 1) * W // NQ)
         name = ("QP", u, g)
 
         def body():
             need("Y%d" % u)
             for lo in range(cs.start, cs.stop, CW):
-                value = dot(whole(yb, u), mem[:, lo : lo + CW])
+                value = dot(whole(yb, u), mh0[:, lo : lo + CW])
                 part2[u, :, :, rs, lo : lo + CW] = value.astype(BF).reshape(2, 4, SH, CW)
 
-        starts, _ = row_job(u, rs, cs, rank, name)
-        deps = [("P", 1, g) for g in range(NJ)] if u == 0 else all_mu
-        task(name, deps, [], 0.6, body, starts, rank)
+        starts, last = row_job(u, rs, cs, rank, name)
+        task(name, [("P", 1, g) for g in range(NJ)], [], 0.6, body, starts, rank)
+
+        return last
 
     for g in range(NQ):
         query_part(0, g, 20 + g)
-        query_part(1, g, 24 + g)
+    q1_sums = [query_part(1, g, 24 + g) for g in range(NQ)]
+
+    def query_update():
+        rank, rs, cs = 16.5, slice(0, SH), slice(0, 128)
+        n = lambda k: ("u", 0, rank, k)
+
+        def body():
+            value = dot(whole(yb, 1), full[1, z].reshape(128, W), NT)
+            upart[...] = value.astype(BF).reshape(2, 4, SH, 128)
+
+        def store(rs, cs, total):
+            ufull[z] = total.astype(BF)
+
+        send_group(("u", 0), rbuf.at[pl.ds(0, 2), pl.ds(0, 5), rs, cs])
+        copy(n("Gp"), "z+", ufull.at[z], ufull.at[z], 1 / 64, ("u", 0))
+        group(n("G"), gbuf.at[0, pl.ds(0, 2)])
+        copy(n("Gm"), "z-", ufull.at[z], ufull.at[z], 1 / 64, ("u", 0), n("G"))
+        copy(n("F"), "z+", ufull.at[zm], ufull.at[zm], 1 / 64, ("u", 0), n("G"))
+        starts, last = reduce_job(
+            "u", 0, rs, cs, rank, lambda i, half: upart.at[half, i], ubuf, ("UP",), y_ring, y_names, store, 0.0,
+            [n("Gp"), n("Gm")],
+        )
+        task(("UP",), ends[1], [], 0.3, body, starts, rank)
+        task(n("s4"), [last], [n("Gp")], 0.05, None, [n("F")], rank)
+
+        def final():
+            lhs = jnp.concatenate([ufull[i] for i in range(4)], axis=1)
+            for g in range(NJ):
+                step = dot(lhs, kb[0, :, :, cols(g)].reshape(8 * SH, CW))
+                qg_ref[0, 1, :, cols(g)] = (0.999 * q1[:, cols(g)] - step).astype(BF)
+            out(0, qg_ref, qg_hbm, 0, 1)
+
+        task(("QF",), [n("s4")] + q1_sums, [n("G")], 0.3, final, [], 32)
+
+    query_update()
 
     def phase_b(q, k, rank):
         b, half = (0, ph0) if q == 2 else (1, mh0)
@@ -527,7 +636,7 @@
                 value = dot(err, mem[:, cols(n)]) - dot(wgt, proj[:, cols(n)])
                 part2[u, :, :, rs, cols(n)] = value.astype(BF).reshape(2, 4, RW, CW)
 
-        starts, _ = row_job(u, rs, full_cols, rank, name)
+        starts, _ = (row_x if (u, k) in ROW_X_FIRST else row_job)(u, rs, full_cols, rank, name)
         deps = [ends[2][k]] + all_pu + all_mu if u == 2 else [ends[3][k]] + all_pu + all_mu
         task(name, deps, [], 0.65, body, starts, rank)
 
@@ -556,10 +665,11 @@
         task(("AL", g), [("AE", h) for h in range(NJ)] + ends[2], [], 0.38, body, [("A", g)], 19)
 
         def total():
-            cf[cs, :] = (qb[g // 2, four].astype(F32) + arec[g // 2, four].astype(F32)).reshape(CW, W)
-            out(3, cf, ig_hbm, cs)
-
-        task(("AT", g), [("AL", g)], [("A", g)], 0.1, total, [], 31)
+            both = qb[g // 2, four].astype(F32) + arec[g // 2, four].astype(F32)
+            ph0[cs, :] = both.astype(BF).reshape(CW, W)
+            out(3, ph0, ig_hbm, cs)
+
+        task(("AT", g), [("AL", g)] + [("KP", 2, k) for k in range(NJ)], [("A", g)], 0.1, total, [], 31)
 
     for g in range(NJ):
         adjoint_early(g)
@@ -572,7 +682,7 @@
         order = [tasks[i] for i in ORDER]
     held = []
     for item in order:
-        if held is not None and (item.groups or len(held) == 6):
+        if held is not None and (item.groups or len(held) == 4):
             pl.semaphore_wait(barrier, len(device))
             for name in [name for early in held for name in early.starts]:
                 copies[name].start()
@@ -588,21 +698,21 @@
             copies[name].start()
     for wait, _ in sends.values():
         wait.wait()
-    for i, (ref, hbm) in enumerate(((qg_ref, qg_hbm), (kg_ref, kg_hbm), (vg_ref, vg_hbm), (cf, ig_hbm))):
+    for i, (ref, hbm) in enumerate(((qg_ref, qg_hbm), (kg_ref, kg_hbm), (vg_ref, vg_hbm), (ph0, ig_hbm))):
         pltpu.make_async_copy(ref, hbm, osem.at[i]).wait()
 
 
 def on_device(query, key, value, out_grad, rate, memory_init, memory_cot):
     shared = (1, 2, 8, SH, W)
     vm = pltpu.VMEM
-    n_recv, n_send = 17 * 7 + (2 * NQ + 8) * 3 + NJ, 10
+    n_recv, n_send = 16 * 7 + 4 + (2 * NQ + 8) * 3 + 5 + NJ, 11
     outs = pl.pallas_call(
         kernel,
         out_shape=(
             jax.ShapeDtypeStruct((1, 2, SH, W), BF),
             jax.ShapeDtypeStruct((1, 2, SH, W), BF),
             jax.ShapeDtypeStruct((1, 2, SH, W), BF),
-            jax.ShapeDtypeStruct((W, W), F32),
+            jax.ShapeDtypeStruct((W, W), BF),
         ),
         in_specs=[pl.BlockSpec(memory_space=pltpu.HBM)] * 7,
         out_specs=(pl.BlockSpec(memory_space=pl.ANY),) * 4,
@@ -632,6 +742,10 @@
             vm((2, 4, SH, 128), BF),
             vm((1, 7, SH, 128), BF),
             vm((2, SH, W), F32),
+            vm((2, 4, SH, 128), BF),
+            vm((4, SH, 128), BF),
+            vm((1, 7, SH, 128), BF),
+            vm((SH, W), F32),
             pltpu.SemaphoreType.DMA((n_send,)),
             pltpu.SemaphoreType.DMA((n_recv,)),
             pltpu.SemaphoreType.DMA((16,)),
@@ -649,30 +763,32 @@
 
 
 def publish_kernel(*refs):
-    ins, outs, held, (rsem, wsem) = refs[:4], refs[4:8], refs[8:12], refs[12:]
-    whole = [(ins[i], held[i], outs[i]) for i in range(3)]
+    ins, outs, held, wide, (rsem, wsem) = refs[:4], refs[4:8], refs[8:12], refs[12], refs[13:]
     rows = [pl.ds(g * 128, 128) for g in range(8)]
-    parts = [(ins[3].at[r], held[3].at[r], outs[3].at[r]) for r in rows] + whole
-    reads = [pltpu.make_async_copy(a, b, rsem.at[i]) for i, (a, b, _) in enumerate(parts)]
-    writes = [pltpu.make_async_copy(b, c, wsem.at[i]) for i, (_, b, c) in enumerate(parts)]
+    reads = [(ins[3].at[r], held[3].at[r]) for r in rows] + [(ins[i], held[i]) for i in range(3)]
+    writes = [(wide.at[r], outs[3].at[r]) for r in rows] + [(held[i], outs[i]) for i in range(3)]
+    reads = [pltpu.make_async_copy(*pair, rsem.at[i]) for i, pair in enumerate(reads)]
+    writes = [pltpu.make_async_copy(*pair, wsem.at[i]) for i, pair in enumerate(writes)]
     for read in reads:
         read.start()
-    for read, write in zip(reads, writes):
+    for i, (read, write) in enumerate(zip(reads, writes)):
         read.wait()
+        if i < 8:
+            wide[rows[i], :] = held[3][rows[i], :].astype(F32)
         write.start()
     for write in writes:
         write.wait()
 
 
 def publish(*arrays):
-    shapes = tuple(jax.ShapeDtypeStruct(a.shape, a.dtype) for a in arrays)
+    shapes = [jax.ShapeDtypeStruct(a.shape, a.dtype) for a in arrays[:3]] + [jax.ShapeDtypeStruct((W, W), F32)]
     return pl.pallas_call(
         publish_kernel,
-        out_shape=shapes,
+        out_shape=tuple(shapes),
         in_specs=[pl.BlockSpec(memory_space=pl.ANY)] * 4,
         out_specs=(pl.BlockSpec(memory_space=pl.ANY),) * 4,
         scratch_shapes=[pltpu.VMEM(a.shape, a.dtype) for a in arrays]
-        + [pltpu.SemaphoreType.DMA((11,)), pltpu.SemaphoreType.DMA((11,))],
+        + [pltpu.VMEM((W, W), F32), pltpu.SemaphoreType.DMA((11,)), pltpu.SemaphoreType.DMA((11,))],
         compiler_params=pltpu.CompilerParams(vmem_limit_bytes=60 * 2**20),
         name="publish",
     )(*arrays)

time: 91.1 us -> 87.6 us (0.962)
  Pallas kernels: 90.2 us -> 86.6 us
    pallas_call x1, Pallas kernels: 85.8 us -> 83.2 us  [on_device(): pl.pallas_call(kernel, out_shape=(jax.ShapeDtypeStruct((1, 2, SH, W), BF)...]
    pallas_call x1, Pallas kernels: 4.35 us -> 3.42 us  [publish(): pl.pallas_call(publish_kernel, out_shape=tuple(shapes), in_specs=[pl.Bloc...]
where the time goes in v3:
time: 87.6 us; the launch traced here: 87.5 us
  Pallas kernels  86.6 us (99%)
    pallas_call x1, Pallas kernels, on_device(): pl.pallas_call(kernel, out_shape=(jax.ShapeDtypeStruct((1, 2, SH, W), BF)...  83.2 us
    pallas_call x1, Pallas kernels, publish(): pl.pallas_call(publish_kernel, out_shape=tuple(shapes), in_specs=[pl.Bloc...  3.42 us

profile of v3, /device:TPU:0, one launch (start us, length us, event | category | flops | bytes accessed | tf_op | source)
XLA Modules:
  0.0 87.5 jit_solution(16267116015671183500)
XLA Ops:
  0.6 83.2 %memory_backward.1 = (bf16[1,2,64,1024]{3,2,1,0:T(8,128)(2,1)}, bf16[1,2,64,1024]{3,2,1,0:T(8,128)(2,1)}, bf16[1,2,64,1024]{3,2,1,0:T(8,128)(2,1)}, bf16[1024,1024]{1,0:T(8,128)(2,1)}) custom-call(bf16[1,2,8,64,1024]{4,3,2,1,0:T(8,128)(2,1)} %bitcast.4, bf16[1,2,8,64,1024]{4,3,2,1,0:T(8,128)(2,1)} %bitcast.5, bf16[1,2,8,64,1024]{4,3,2,1,0:T(8,128)(2,1)} %bitcast.6, ...), custom_call_target="tpu_custom_call" | custom-call | tf_op jit(solution)/shard_map/memory_backward/pallas_call | solution.py:709
  83.9 3.4 %publish.1 = (bf16[1,2,64,1024]{3,2,1,0:T(8,128)(2,1)}, bf16[1,2,64,1024]{3,2,1,0:T(8,128)(2,1)}, bf16[1,2,64,1024]{3,2,1,0:T(8,128)(2,1)}, f32[1024,1024]{1,0:T(8,128)}) custom-call(bf16[1,2,64,1024]{3,2,1,0:T(8,128)(2,1)} %get-tuple-element.8.refs_0_, bf16[1,2,64,1024]{3,2,1,0:T(8,128)(2,1)} %get-tuple-element.9.refs_1_, ...), custom_call_target="tpu_custom_call" | custom-call | tf_op jit(solution)/shard_map/publish/pallas_call | solution.py:785

commit v4 on v3

--- a/solution.py
+++ b/solution.py
@@ -90,6 +90,10 @@
         "dp": (1 - dp, row, col),
     }
 
+    barrier = pltpu.get_barrier_semaphore()
+    for partner in device.values():
+        pl.semaphore_signal(barrier, inc=1, device_id=partner, device_id_type=MESH)
+
     loads = {}
 
     def load(name, src, dst):
@@ -133,10 +137,6 @@
                 next_stage()
 
     next_stage()
-
-    barrier = pltpu.get_barrier_semaphore()
-    for partner in device.values():
-        pl.semaphore_signal(barrier, inc=1, device_id=partner, device_id_type=MESH)
 
     def rates():
         need("R")
@@ -682,7 +682,7 @@
         order = [tasks[i] for i in ORDER]
     held = []
     for item in order:
-        if held is not None and (item.groups or len(held) == 4):
+        if held is not None and (item.groups or len(held) == 2):
             pl.semaphore_wait(barrier, len(device))
             for name in [name for early in held for name in early.starts]:
                 copies[name].start()
@@ -765,16 +765,16 @@
 def publish_kernel(*refs):
     ins, outs, held, wide, (rsem, wsem) = refs[:4], refs[4:8], refs[8:12], refs[12], refs[13:]
     rows = [pl.ds(g * 128, 128) for g in range(8)]
-    reads = [(ins[3].at[r], held[3].at[r]) for r in rows] + [(ins[i], held[i]) for i in range(3)]
-    writes = [(wide.at[r], outs[3].at[r]) for r in rows] + [(held[i], outs[i]) for i in range(3)]
+    reads = [(ins[i], held[i]) for i in range(3)] + [(ins[3].at[r], held[3].at[r]) for r in rows]
+    writes = [(held[i], outs[i]) for i in range(3)] + [(wide.at[r], outs[3].at[r]) for r in rows]
     reads = [pltpu.make_async_copy(*pair, rsem.at[i]) for i, pair in enumerate(reads)]
     writes = [pltpu.make_async_copy(*pair, wsem.at[i]) for i, pair in enumerate(writes)]
     for read in reads:
         read.start()
     for i, (read, write) in enumerate(zip(reads, writes)):
         read.wait()
-        if i < 8:
-            wide[rows[i], :] = held[3][rows[i], :].astype(F32)
+        if i >= 3:
+            wide[rows[i - 3], :] = held[3][rows[i - 3], :].astype(F32)
         write.start()
     for write in writes:
         write.wait()

time: 87.6 us -> 87.7 us (level)
  no operation moved by 1% of the time
where the time goes in v4:
time: 87.7 us; the launch traced here: 87.6 us
  Pallas kernels  86.7 us (99%)
    pallas_call x1, Pallas kernels, on_device(): pl.pallas_call(kernel, out_shape=(jax.ShapeDtypeStruct((1, 2, SH, W), BF)...  83.3 us
    pallas_call x1, Pallas kernels, publish(): pl.pallas_call(publish_kernel, out_shape=tuple(shapes), in_specs=[pl.Bloc...  3.42 us

profile of v4, /device:TPU:0, one launch (start us, length us, event | category | flops | bytes accessed | tf_op | source)
XLA Modules:
  0.0 87.6 jit_solution(16323053919029607168)
XLA Ops:
  0.6 83.3 %memory_backward.1 = (bf16[1,2,64,1024]{3,2,1,0:T(8,128)(2,1)}, bf16[1,2,64,1024]{3,2,1,0:T(8,128)(2,1)}, bf16[1,2,64,1024]{3,2,1,0:T(8,128)(2,1)}, bf16[1024,1024]{1,0:T(8,128)(2,1)}) custom-call(bf16[1,2,8,64,1024]{4,3,2,1,0:T(8,128)(2,1)} %bitcast.4, bf16[1,2,8,64,1024]{4,3,2,1,0:T(8,128)(2,1)} %bitcast.5, bf16[1,2,8,64,1024]{4,3,2,1,0:T(8,128)(2,1)} %bitcast.6, ...), custom_call_target="tpu_custom_call" | custom-call | tf_op jit(solution)/shard_map/memory_backward/pallas_call | solution.py:709
  84.0 3.4 %publish.1 = (bf16[1,2,64,1024]{3,2,1,0:T(8,128)(2,1)}, bf16[1,2,64,1024]{3,2,1,0:T(8,128)(2,1)}, bf16[1,2,64,1024]{3,2,1,0:T(8,128)(2,1)}, f32[1024,1024]{1,0:T(8,128)}) custom-call(bf16[1,2,64,1024]{3,2,1,0:T(8,128)(2,1)} %get-tuple-element.8.refs_0_, bf16[1,2,64,1024]{3,2,1,0:T(8,128)(2,1)} %get-tuple-element.9.refs_1_, ...), custom_call_target="tpu_custom_call" | custom-call | tf_op jit(solution)/shard_map/publish/pallas_call | solution.py:785
